TPU v7x, 256 devices: a whole 4x4x8 slice. The times are simulated.
256 devices in a mesh: head: 4 (over z_hi, core), inner: 16 (over x, y), outer: 4 (over z_lo).
Axes of the slice: x: 4, y: 4, z: 8 (z_hi: 2, z_lo: 4; z = z_hi * 4 + z_lo), core: 2. Of those that a mesh axis runs over, the one named last changes fastest.
Arguments:
- query: bfloat16 [32768, 3584], P(('head', 'inner', 'outer')), may hold values from -24 to 24
- key: bfloat16 [32768, 512], P(('head', 'inner', 'outer')), may hold values from -9 to 9
- value: bfloat16 [32768, 512], P(('head', 'inner', 'outer')), may hold values from -6 to 6
- vertical_blocks: int32 [4, 8], replicated, may hold values from 0 to 511, as said below
- slash_offsets: int32 [4, 9], replicated, may hold values from 0 to 8, as said below
- block_counts: int32 [4, 2], replicated, may hold values from 1 to 9, as said below
Outputs:
- attended: bfloat16 [32768, 3584], P(('head', 'inner', 'outer'))
Inputs may be any that keep to these rules, and one draw needn't show every extreme that they name: `vertical_blocks`: within a row the entries are distinct indices of 64-token blocks; only the first block_counts[h, 0] of row h are used. `slash_offsets`: within a row the entries are distinct and the first is 0; only the first block_counts[h, 1] of row h are used. `block_counts`: column 0 is at most 8, column 1 at most 9.
All inputs are finite; a program needn't handle non-finite values.
Results may differ from a plain program's by a relative error of at most 0.0044.
Values may be sent and summed in bfloat16 or wider, within the bound.
No kernel may reach another device: no remote copies, remote signals or barrier semaphores. Data moves between devices by JAX's collectives and lax.ppermute only.
A program may use at most 64 MiB of HBM per device.

v0:
```python
import jax
import jax.numpy as jnp
from jax import lax
from jax.sharding import PartitionSpec as P

QH = 28
KVH = 4
HD = 128
BLOCK = 64
MAXV = 8
SLASH_REACH = 8
MAXS = 9


NEGATIVE = -1e30


def shifted(block, axis, distance):
    devices = range(lax.axis_size(axis))
    route = [(i - distance, i) for i in devices if i - distance in devices]
    return lax.ppermute(block, axis, route)


def stack_pairs(keys_in, values_in, groups):
    shape = keys_in.shape[:-1] + (groups, HD)
    return jnp.concatenate([keys_in.reshape(shape), values_in.reshape(shape)], axis=-1)


def owned_blocks(stacked, vertical, local_blocks, contexts, context):
    pieces_count = stacked.shape[0]
    groups = stacked.shape[2]
    flat_blocks = stacked.reshape(pieces_count * local_blocks, BLOCK, groups, 2 * HD)
    shard_ids = vertical // local_blocks
    owner_ids = shard_ids % contexts
    position = shard_ids // contexts * local_blocks + vertical % local_blocks
    gathered = flat_blocks[position]
    diagonal = jnp.stack([gathered[g, :, :, g] for g in range(groups)], axis=0)
    holder = (owner_ids == context)[:, :, None, None]
    owned = jnp.where(holder, diagonal, jnp.zeros_like(diagonal))
    return owned.reshape(groups * MAXV * BLOCK, 2 * HD).astype(jnp.float32)


def attend(queries, stacked, earlier, vertical_pairs, vertical, offsets, counts, block_ids):
    pieces_count = stacked.shape[0]
    tokens = stacked.shape[1]
    groups = stacked.shape[2]
    local_blocks = tokens // BLOCK
    per_group = QH // KVH
    span_blocks = SLASH_REACH + local_blocks
    total_blocks = pieces_count * local_blocks
    step_blocks = min(8, total_blocks)
    extended = jnp.concatenate([earlier, stacked], axis=1).reshape(
        pieces_count * span_blocks, BLOCK, groups, 2 * HD
    )
    slash_sources = [extended[:, :, g] for g in range(groups)]
    query_blocks = queries.reshape(total_blocks, BLOCK, groups, per_group, HD)
    serial = jnp.arange(total_blocks, dtype=jnp.int32)
    anchors = serial // local_blocks * span_blocks + SLASH_REACH + serial % local_blocks
    flat_ids = block_ids.reshape(total_blocks)
    vertical_pairs = vertical_pairs.reshape(groups, MAXV * BLOCK, 2 * HD)
    within = jnp.arange(BLOCK, dtype=jnp.int32)
    scale = HD ** (-0.5)

    def one_group(group):
        query_pos = flat_ids[:, None] * BLOCK + within[None, :]
        results = []
        for g in range(groups):
            vertical_live = (jnp.arange(MAXV, dtype=jnp.int32) < counts[g, 0])[None, :] & (
                vertical[g][None, :] <= flat_ids[:, None]
            )
            slash_ids = flat_ids[:, None] - offsets[g][None, :]
            doubled = jnp.any(
                (slash_ids[:, :, None] == vertical[g][None, None, :]) & vertical_live[:, None, :],
                axis=2,
            )
            slash_live = (
                (jnp.arange(MAXS, dtype=jnp.int32) < counts[g, 1])[None, :]
                & (slash_ids >= 0)
                & jnp.logical_not(doubled)
            )
            local_index = jnp.clip(
                anchors[:, None] - offsets[g][None, :], 0, pieces_count * span_blocks - 1
            )
            slash_pairs = slash_sources[g][local_index]
            slash_keys = slash_pairs[..., :HD].reshape(step_blocks, MAXS * BLOCK, HD)
            slash_values = slash_pairs[..., HD:].reshape(step_blocks, MAXS * BLOCK, HD)
            vertical_pos = (vertical[g][:, None] * BLOCK + within[None, :]).reshape(MAXV * BLOCK)
            slash_pos = (slash_ids[:, :, None] * BLOCK + within[None, None, :]).reshape(
                step_blocks, MAXS * BLOCK
            )
            vertical_allowed = (
                jnp.repeat(vertical_live, BLOCK, axis=1)[:, None, :]
                & (vertical_pos[None, None, :] <= query_pos[:, :, None])
            )[:, :, None, :]
            slash_allowed = (
                jnp.repeat(slash_live, BLOCK, axis=1)[:, None, :]
                & (slash_pos[:, None, :] <= query_pos[:, :, None])
            )[:, :, None, :]
            heads_here = query_blocks[:, :, g]
            vertical_scores = (
                jnp.einsum(
                    "qbrd,nd->qbrn",
                    heads_here,
                    vertical_pairs[g, :, :HD],
                    preferred_element_type=jnp.float32,
                )
                * scale
            )
            slash_scores = (
                jnp.einsum(
                    "qbrd,qnd->qbrn", heads_here, slash_keys, preferred_element_type=jnp.float32
                )
                * scale
            )
            highest = jnp.maximum(
                jnp.max(
                    jnp.where(vertical_allowed, vertical_scores, NEGATIVE), axis=-1, keepdims=True
                ),
                jnp.max(jnp.where(slash_allowed, slash_scores, NEGATIVE), axis=-1, keepdims=True),
            )
            vertical_weights = jnp.where(vertical_allowed, jnp.exp(vertical_scores - highest), 0.0)
            slash_weights = jnp.where(slash_allowed, jnp.exp(slash_scores - highest), 0.0)
            totals = jnp.sum(vertical_weights, axis=-1) + jnp.sum(slash_weights, axis=-1)
            attended = jnp.einsum(
                "qbrn,nd->qbrd",
                vertical_weights.astype(jnp.bfloat16),
                vertical_pairs[g, :, HD:],
                preferred_element_type=jnp.float32,
            )
            attended = attended + jnp.einsum(
                "qbrn,qnd->qbrd",
                slash_weights.astype(jnp.bfloat16),
                slash_values,
                preferred_element_type=jnp.float32,
            )
            results.append((attended / totals[..., None]).astype(jnp.bfloat16))
        return jnp.stack(results, axis=2)

    mixture = lax.map(one_group, jnp.arange(total_blocks // step_blocks, dtype=jnp.int32))
    return mixture.reshape(pieces_count, tokens, groups * per_group * HD)


def local(query, key, value, vertical_blocks, slash_offsets, block_counts):
    tokens = query.shape[0]
    local_blocks = tokens // BLOCK
    rim_rows = SLASH_REACH * BLOCK
    reach = (rim_rows + tokens - 1) // tokens
    stacked = stack_pairs(key[None], value[None], KVH)
    contexts = lax.axis_size(("head", "inner", "outer"))
    context = lax.axis_index(("head", "inner", "outer"))
    behind = []
    for distance in range(reach, 0, -1):
        behind.append(shifted(stacked, ("head", "inner", "outer"), distance))
    earlier = jnp.concatenate(behind, axis=1)
    contribution = owned_blocks(stacked, vertical_blocks, local_blocks, contexts, context)
    vertical_pairs = lax.psum(contribution, ("head", "inner", "outer")).astype(jnp.bfloat16)
    piece_ids = (context * local_blocks + jnp.arange(local_blocks, dtype=jnp.int32))[None, :]
    attended = attend(
        query[None],
        stacked,
        earlier,
        vertical_pairs,
        vertical_blocks,
        slash_offsets,
        block_counts,
        piece_ids,
    )
    result = attended[0]
    return result


def solution(mesh):
    placed = (
        P(("head", "inner", "outer"), None),
        P(("head", "inner", "outer"), None),
        P(("head", "inner", "outer"), None),
        P(),
        P(),
        P(),
    )
    return jax.shard_map(
        local,
        mesh=mesh,
        in_specs=placed,
        out_specs=P(("head", "inner", "outer"), None),
        check_vma=False,
    )
```

profile of v0, /device:TPU:1, one launch (start us, length us, event | category | flops | bytes accessed | tf_op | source)
XLA Modules:
  0.0 200.3 jit_solution(9845250740187476322)
XLA Ops:
  0.0 1.0 reshape_broadcast_in_dim.10
  1.7 0.7 copy_dynamic-update-slice_fusion.3
  2.4 0.9 reshape_broadcast_in_dim.11
  3.3 0.7 copy_dynamic-update-slice_fusion.1
  4.0 4.0 %collective-permute-start = (bf16[1,128,4,256]{3,1,2,0:T(8,128)(2,1)}, bf16[1,128,4,256]{3,1,2,0:T(8,128)(2,1)}, u32[]{:S(2)}, u32[]{:S(2)}) collective-permute-start(bf16[1,128,4,256]{3,1,2,0:T(8,128)(2,1)} %copy_dynamic-update-slice_fusion.1), channel_id=1, source_target_pairs={{0,4},{1,5},{2,6},{3,7},{4,8},{5,9},{6,10},{7,11},{8,12},{9,13},{1... | collective-permute-start | bytes 786440 | tf_op jit(solution)/shard_map/ppermute | solution.py:21
  8.1 6.3 %collective-permute-start.1 = (bf16[1,128,4,256]{3,1,2,0:T(8,128)(2,1)}, bf16[1,128,4,256]{3,1,2,0:T(8,128)(2,1)}, u32[]{:S(2)}, u32[]{:S(2)}) collective-permute-start(bf16[1,128,4,256]{3,1,2,0:T(8,128)(2,1)} %copy_dynamic-update-slice_fusion.1), channel_id=1, source_target_pairs={{0,3},{1,4},{2,5},{3,6},{4,7},{5,8},{6,9},{7,10},{8,11},{9,12},{10... | collective-permute-start | bytes 786440 | tf_op jit(solution)/shard_map/ppermute | solution.py:21
  14.3 1.9 collective-permute-start.2
  16.3 3.0 %collective-permute-start.3 = (bf16[1,128,4,256]{3,1,2,0:T(8,128)(2,1)}, bf16[1,128,4,256]{3,1,2,0:T(8,128)(2,1)}, u32[]{:S(2)}, u32[]{:S(2)}) collective-permute-start(bf16[1,128,4,256]{3,1,2,0:T(8,128)(2,1)} %copy_dynamic-update-slice_fusion.1), channel_id=1, source_target_pairs={{0,1},{1,2},{2,3},{3,4},{4,5},{5,6},{6,7},{7,8},{8,9},{9,10},{10,1... | collective-permute-start | bytes 786440 | tf_op jit(solution)/shard_map/ppermute | solution.py:21
  19.3 0.8 broadcast_multiply_fusion.4
  20.1 0.8 slice_bitcast_fusion.27
  21.0 0.9 concatenate.14
  21.9 0.9 concatenate.13
  22.9 0.7 compare_select_fusion
  24.1 0.7 fusion.105
  25.6 1.6 fusion.135
  27.2 1.2 iota_compare_fusion.5
  28.4 1.3 iota_compare_fusion.1
  33.0 1.1 reshape_broadcast_in_dim.9
  34.1 1.0 fusion.130
  35.4 5.7 %gather_fusion = bf16[32,64,4,256]{3,2,1,0:T(4,128)(2,1)} fusion(bf16[2,64,4,256]{3,2,1,0:T(4,128)(2,1)S(1)} %pad_maximum_fusion.2, s32[1024]{0:T(1024)S(1)} %pad_clamp_fusion.4), kind=kCustom, calls=%fused_computation | custom fusion | bytes 8388736 | tf_op jit(solution)/shard_map/gather | solution.py:36
  41.1 3.8 %fusion.129 = (bf16[1,8,64,1,256]{4,3,2,1,0:T(2,128)(2,1)S(1)}, bf16[1,8,64,1,256]{4,3,2,1,0:T(2,128)(2,1)S(1)}, bf16[1,8,64,1,256]{4,3,2,1,0:T(2,128)(2,1)S(1)}, bf16[1,8,64,1,256]{4,3,2,1,0:T(2,128)(2,1)S(1)}) fusion(bf16[4,8,64,4,256]{4,3,2,1,0:T(4,128)(2,1)} %bitcast.331), kind=kLoop, calls=%fused_computation.266 | loop fusion | bytes 2097152 | tf_op jit(solution)/shard_map/slice | solution.py:37
  45.7 89.4 %all-reduce.1 = bf16[2048,256]{1,0:T(8,128)(2,1)S(1)} all-reduce(f32[2048,256]{1,0:T(8,128)S(1)} %fusion.72), channel_id=1, replica_groups=mesh['head'=4,'inner'=16,'outer'=4] {'head','inner','outer'}, use_global_device_ids=true, to_apply=%region_0.1 | all-reduce | flops 524288 | bytes 3145728 | tf_op jit(solution)/shard_map/psum | solution.py:156
  135.2 1.0 slice_bitcast_fusion.26
  136.1 0.7 broadcast_subtract_fusion.3
  137.5 0.8 and_reduce_fusion.3
  138.3 0.8 and_reduce_fusion
  139.1 0.8 and_reduce_fusion.1
  139.8 0.8 and_reduce_fusion.2
  140.6 1.2 iota_compare_fusion.4
  141.8 1.3 iota_compare_fusion
  143.1 0.7 not_and_fusion.3
  144.4 0.9 compare_and_fusion.7
  145.4 3.3 %fusion.12 = (f32[2,64,7]{1,2,0:T(8,128)}, f32[512,2,64,7]{0,2,3,1:T(8,128)}) fusion(pred[2,64,512]{2,1,0:T(8,128)(4,1)S(1)} %get-tuple-element.100, bf16[2,64,1,7,128]{4,3,2,1,0:T(8,128)(2,1)} %get-tuple-element.56, bf16[4,512,256]{2,1,0:T(8,128)(2,1)S(1)} %bitcast.332), kind=kOutput, calls=%fused_computation.27 | convolution fusion | flops 118815872 | bytes 2264576 | tf_op jit(solution)/shard_map/while/body/eval_jaxpr/qbrd,nd->qbrn/dot_general | solution.py:101
  148.8 1.6 fusion.15
  150.4 1.8 fusion.18
  152.2 2.3 %fusion.21 = (f32[2,64,7]{1,2,0:T(8,128)}, f32[512,2,64,7]{0,2,3,1:T(8,128)}) fusion(pred[2,64,512]{2,1,0:T(8,128)(4,1)S(1)} %get-tuple-element.97, bf16[2,64,1,7,128]{4,3,2,1,0:T(8,128)(2,1)S(1)} %get-tuple-element.39, bf16[4,512,256]{2,1,0:T(8,128)(2,1)S(1)} %bitcast.335), kind=kOutput, calls=%fused_computation.42 | convolution fusion | flops 118815872 | bytes 2297344 | tf_op jit(solution)/shard_map/while/body/eval_jaxpr/qbrd,nd->qbrn/dot_general | solution.py:101
  154.5 1.1 compare_and_fusion.3
  157.2 1.0 constant_dynamic-update-slice_fusion.3
  158.2 1.0 constant_dynamic-update-slice_fusion.2
  159.2 1.0 constant_dynamic-update-slice_fusion.1
  160.2 1.0 constant_dynamic-update-slice_fusion
  162.0 0.9 fusion.134
  162.9 1.6 fusion
  164.6 2.2 %fusion.73 = f32[2,64,7,128]{3,1,2,0:T(8,128)} fusion(f32[512,2,64,7]{0,2,3,1:T(8,128)S(1)} %copy-done.5, f32[2,64,7]{1,2,0:T(8,128)S(1)} %max.53, pred[2,64,512]{2,1,0:T(8,128)(4,1)S(1)} %copy-done.27, bf16[4,512,256]{2,1,0:T(8,128)(2,1)} %bitcast.336), kind=kOutput, calls=%fused_computation.96 | convolution fusion | flops 119275520 | bytes 2493952 | tf_op jit(solution)/shard_map/while/body/eval_jaxpr/qbrn,nd->qbrd/dot_general | solution.py:124
  166.8 1.2 fusion.38
  168.0 1.6 gather_fusion.3
  169.5 2.0 fusion.133
  171.5 2.8 %fusion.3 = (f32[2,64,7]{1,2,0:T(8,128)S(1)}, f32[2,576,64,7]{1,2,3,0:T(8,128)}) fusion(pred[2,64,576]{2,1,0:T(8,128)(4,1)} %get-tuple-element.85, bf16[2,576,128,1]{2,1,3,0:T(8,128)(2,1)S(1)} %bitcast.347, bf16[2,64,1,7,128]{4,3,2,1,0:T(8,128)(2,1)S(1)} %copy-done.10), kind=kOutput, calls=%fused_computation.12 | convolution fusion | flops 133667968 | bytes 2665984 | tf_op jit(solution)/shard_map/while/body/eval_jaxpr/qbrd,qnd->qbrn/dot_general | solution.py:110
  174.3 2.2 %fusion.75 = f32[2,64,7,128]{3,1,2,0:T(8,128)} fusion(f32[512,2,64,7]{0,2,3,1:T(8,128)S(1)} %copy-done.4, f32[2,64,7]{1,2,0:T(8,128)S(1)} %max.52, pred[2,64,512]{2,1,0:T(8,128)(4,1)S(1)} %copy-done.25, bf16[4,512,256]{2,1,0:T(8,128)(2,1)} %bitcast.337), kind=kOutput, calls=%fused_computation.97 | convolution fusion | flops 119275520 | bytes 2493952 | tf_op jit(solution)/shard_map/while/body/eval_jaxpr/qbrn,nd->qbrd/dot_general | solution.py:124
  176.5 1.2 fusion.36
  177.7 0.7 gather_fusion.2
  178.5 0.9 fusion.132
  179.4 2.9 %fusion.6 = (f32[2,64,7]{1,2,0:T(8,128)S(1)}, f32[2,576,64,7]{1,2,3,0:T(8,128)}) fusion(pred[2,64,576]{2,1,0:T(8,128)(4,1)} %get-tuple-element.84, bf16[2,576,128,1]{2,1,3,0:T(8,128)(2,1)S(1)} %bitcast.348, bf16[2,64,1,7,128]{4,3,2,1,0:T(8,128)(2,1)} %get-tuple-element.41), kind=kOutput, calls=%fused_computation.17 | convolution fusion | flops 133667968 | bytes 2665984 | tf_op jit(solution)/shard_map/while/body/eval_jaxpr/qbrd,qnd->qbrn/dot_general | solution.py:110
  182.3 2.2 %fusion.77 = f32[2,64,7,128]{3,1,2,0:T(8,128)} fusion(f32[512,2,64,7]{0,2,3,1:T(8,128)S(1)} %copy-done.3, f32[2,64,7]{1,2,0:T(8,128)S(1)} %max.51, pred[2,64,512]{2,1,0:T(8,128)(4,1)S(1)} %copy-done.23, bf16[4,512,256]{2,1,0:T(8,128)(2,1)} %bitcast.338), kind=kOutput, calls=%fused_computation.98 | convolution fusion | flops 119275520 | bytes 2493952 | tf_op jit(solution)/shard_map/while/body/eval_jaxpr/qbrn,nd->qbrd/dot_general | solution.py:124
  184.5 1.2 fusion.34
  185.7 0.7 gather_fusion.1
  187.2 0.7 copy-done.2
  187.9 1.4 fusion.79
  190.1 0.7 fusion.30
  191.1 0.7 fusion.28
  192.0 1.0 fusion.26
  192.9 0.7 fusion.24
  196.3 0.7 fusion.49
  198.4 1.9 squeeze_reshape.3
  (188 shorter events, 15.9 us)
Async XLA Ops:
  0.0 33.0 %copy-start.15 = (bf16[128,3584]{1,0:T(8,128)(2,1)S(1)}, bf16[128,3584]{1,0:T(8,128)(2,1)}, u32[]{:S(2)}) copy-start(bf16[128,3584]{1,0:T(8,128)(2,1)} %param.6) | copy-start | bytes 2752516
  1.0 0.7 copy-start.13
  3.3 29.7 %copy-start.11 = (bf16[1,128,4,128]{3,2,1,0:T(4,128)(2,1)}, bf16[1,128,4,128]{3,2,1,0:T(4,128)(2,1)S(1)}, u32[]{:S(2)}) copy-start(bf16[1,128,4,128]{3,2,1,0:T(4,128)(2,1)S(1)} %reshape_broadcast_in_dim.11) | copy-start | bytes 393220
  4.0 153.2 %collective-permute-start = (bf16[1,128,4,256]{3,1,2,0:T(8,128)(2,1)}, bf16[1,128,4,256]{3,1,2,0:T(8,128)(2,1)}, u32[]{:S(2)}, u32[]{:S(2)}) collective-permute-start(bf16[1,128,4,256]{3,1,2,0:T(8,128)(2,1)} %copy_dynamic-update-slice_fusion.1), channel_id=1, source_target_pairs={{0,4},{1,5},{2,6},{3,7},{4,8},{5,9},{6,10},{7,11},{8,12},{9,13},{1... | collective-permute-start | bytes 786440 | tf_op jit(solution)/shard_map/ppermute | solution.py:21
  8.1 150.1 %collective-permute-start.1 = (bf16[1,128,4,256]{3,1,2,0:T(8,128)(2,1)}, bf16[1,128,4,256]{3,1,2,0:T(8,128)(2,1)}, u32[]{:S(2)}, u32[]{:S(2)}) collective-permute-start(bf16[1,128,4,256]{3,1,2,0:T(8,128)(2,1)} %copy_dynamic-update-slice_fusion.1), channel_id=1, source_target_pairs={{0,3},{1,4},{2,5},{3,6},{4,7},{5,8},{6,9},{7,10},{8,11},{9,12},{10... | collective-permute-start | bytes 786440 | tf_op jit(solution)/shard_map/ppermute | solution.py:21
  14.3 144.8 %collective-permute-start.2 = (bf16[1,128,4,256]{3,1,2,0:T(8,128)(2,1)}, bf16[1,128,4,256]{3,1,2,0:T(8,128)(2,1)}, u32[]{:S(2)}, u32[]{:S(2)}) collective-permute-start(bf16[1,128,4,256]{3,1,2,0:T(8,128)(2,1)} %copy_dynamic-update-slice_fusion.1), channel_id=1, source_target_pairs={{0,2},{1,3},{2,4},{3,5},{4,6},{5,7},{6,8},{7,9},{8,10},{9,11},{10,... | collective-permute-start | bytes 786440 | tf_op jit(solution)/shard_map/ppermute | solution.py:21
  16.3 143.9 %collective-permute-start.3 = (bf16[1,128,4,256]{3,1,2,0:T(8,128)(2,1)}, bf16[1,128,4,256]{3,1,2,0:T(8,128)(2,1)}, u32[]{:S(2)}, u32[]{:S(2)}) collective-permute-start(bf16[1,128,4,256]{3,1,2,0:T(8,128)(2,1)} %copy_dynamic-update-slice_fusion.1), channel_id=1, source_target_pairs={{0,1},{1,2},{2,3},{3,4},{4,5},{5,6},{6,7},{7,8},{8,9},{9,10},{10,1... | collective-permute-start | bytes 786440 | tf_op jit(solution)/shard_map/ppermute | solution.py:21
  21.0 8.8 %copy-start.46 = (s32[8]{0:T(128)}, s32[8]{0:T(128)S(1)}, u32[]{:S(2)}) copy-start(s32[8]{0:T(128)S(1)} %get-tuple-element.76) | copy-start | bytes 100
  21.0 14.1 %copy-start.47 = (s32[8]{0:T(128)}, s32[8]{0:T(128)S(1)}, u32[]{:S(2)}) copy-start(s32[8]{0:T(128)S(1)} %get-tuple-element.78) | copy-start | bytes 100
  21.0 14.1 %copy-start.48 = (s32[8]{0:T(128)}, s32[8]{0:T(128)S(1)}, u32[]{:S(2)}) copy-start(s32[8]{0:T(128)S(1)} %get-tuple-element.77) | copy-start | bytes 100
  21.0 14.1 %copy-start.49 = (s32[8]{0:T(128)}, s32[8]{0:T(128)S(1)}, u32[]{:S(2)}) copy-start(s32[8]{0:T(128)S(1)} %get-tuple-element.75) | copy-start | bytes 100
  24.8 10.3 %copy-start.50 = (s32[2]{0:T(128)}, s32[2]{0:T(128)S(1)}, u32[]{:S(2)}) copy-start(s32[2]{0:T(128)S(1)} %get-tuple-element.141) | copy-start | bytes 28
  29.7 5.4 %copy-start.42 = (pred[2,8]{1,0:T(4,128)(4,1)}, pred[2,8]{1,0:T(4,128)(4,1)S(1)}, u32[]{:S(2)}) copy-start(pred[2,8]{1,0:T(4,128)(4,1)S(1)} %get-tuple-element.124) | copy-start | bytes 52
  29.7 5.4 %copy-start.43 = (pred[2,8]{1,0:T(4,128)(4,1)}, pred[2,8]{1,0:T(4,128)(4,1)S(1)}, u32[]{:S(2)}) copy-start(pred[2,8]{1,0:T(4,128)(4,1)S(1)} %get-tuple-element.122) | copy-start | bytes 52
  29.7 5.4 %copy-start.44 = (pred[2,8]{1,0:T(4,128)(4,1)}, pred[2,8]{1,0:T(4,128)(4,1)S(1)}, u32[]{:S(2)}) copy-start(pred[2,8]{1,0:T(4,128)(4,1)S(1)} %get-tuple-element.123) | copy-start | bytes 52
  29.8 5.4 %copy-start.45 = (pred[2,8]{1,0:T(4,128)(4,1)}, pred[2,8]{1,0:T(4,128)(4,1)S(1)}, u32[]{:S(2)}) copy-start(pred[2,8]{1,0:T(4,128)(4,1)S(1)} %get-tuple-element.121) | copy-start | bytes 52
  35.1 117.1 %copy-start.7 = (bf16[2,64,1,7,128]{4,3,2,1,0:T(8,128)(2,1)}, bf16[2,64,1,7,128]{4,3,2,1,0:T(8,128)(2,1)S(1)}, u32[]{:S(2)}) copy-start(bf16[2,64,1,7,128]{4,3,2,1,0:T(8,128)(2,1)S(1)} %get-tuple-element.39) | copy-start | bytes 688132
  135.2 17.0 %copy-start.6 = (bf16[2048,256]{1,0:T(8,128)(2,1)}, bf16[2048,256]{1,0:T(8,128)(2,1)S(1)}, u32[]{:S(2)}) copy-start(bf16[2048,256]{1,0:T(8,128)(2,1)S(1)} %all-reduce.1) | copy-start | bytes 3145732
  135.2 13.6 %copy-start.10 = (bf16[2,64,1,7,128]{4,3,2,1,0:T(8,128)(2,1)S(1)}, bf16[2,64,1,7,128]{4,3,2,1,0:T(8,128)(2,1)}, u32[]{:S(2)}) copy-start(bf16[2,64,1,7,128]{4,3,2,1,0:T(8,128)(2,1)} %get-tuple-element.40) | copy-start | bytes 688132
  145.4 5.0 %copy-start.24 = (pred[2,64,512]{2,1,0:T(8,128)(4,1)}, pred[2,64,512]{2,1,0:T(8,128)(4,1)S(1)}, u32[]{:S(2)}) copy-start(pred[2,64,512]{2,1,0:T(8,128)(4,1)S(1)} %get-tuple-element.99) | copy-start | bytes 196612
  145.4 5.0 %copy-start.26 = (pred[2,64,512]{2,1,0:T(8,128)(4,1)}, pred[2,64,512]{2,1,0:T(8,128)(4,1)S(1)}, u32[]{:S(2)}) copy-start(pred[2,64,512]{2,1,0:T(8,128)(4,1)S(1)} %get-tuple-element.100) | copy-start | bytes 196612
  145.4 5.0 %copy-start.22 = (pred[2,64,512]{2,1,0:T(8,128)(4,1)}, pred[2,64,512]{2,1,0:T(8,128)(4,1)S(1)}, u32[]{:S(2)}) copy-start(pred[2,64,512]{2,1,0:T(8,128)(4,1)S(1)} %get-tuple-element.98) | copy-start | bytes 196612
  145.4 6.8 %copy-start.20 = (pred[2,64,512]{2,1,0:T(8,128)(4,1)}, pred[2,64,512]{2,1,0:T(8,128)(4,1)S(1)}, u32[]{:S(2)}) copy-start(pred[2,64,512]{2,1,0:T(8,128)(4,1)S(1)} %get-tuple-element.97) | copy-start | bytes 196612
  145.4 5.0 %copy-start.9 = (bf16[2,64,1,7,128]{4,3,2,1,0:T(8,128)(2,1)S(1)}, bf16[2,64,1,7,128]{4,3,2,1,0:T(8,128)(2,1)}, u32[]{:S(2)}) copy-start(bf16[2,64,1,7,128]{4,3,2,1,0:T(8,128)(2,1)} %get-tuple-element.41) | copy-start | bytes 688132
  150.4 4.1 %copy-start.51 = (s32[2,64]{1,0:T(2,128)S(1)}, s32[2,64]{1,0:T(2,128)}, u32[]{:S(2)}) copy-start(s32[2,64]{1,0:T(2,128)} %iota_add_fusion.4) | copy-start | bytes 1540
  152.2 3.4 %copy-start.52 = (s32[2]{0:T(128)S(1)}, s32[2]{0:T(128)}, u32[]{:S(2)}) copy-start(s32[2]{0:T(128)} %fusion.110) | copy-start | bytes 28
  154.5 6.6 %copy-start.14 = (bf16[1,128,4,128]{3,2,1,0:T(4,128)(2,1)S(1)}, bf16[1,128,4,128]{3,2,1,0:T(4,128)(2,1)}, u32[]{:S(2)}) copy-start(bf16[1,128,4,128]{3,2,1,0:T(4,128)(2,1)} %copy-done.13) | copy-start | bytes 393220
  154.5 6.7 %copy-start.12 = (bf16[1,128,4,128]{3,2,1,0:T(4,128)(2,1)S(1)}, bf16[1,128,4,128]{3,2,1,0:T(4,128)(2,1)}, u32[]{:S(2)}) copy-start(bf16[1,128,4,128]{3,2,1,0:T(4,128)(2,1)} %copy-done.11) | copy-start | bytes 393220
  162.0 2.5 %copy-start.38 = (f32[2,64,7]{1,2,0:T(8,128)S(1)}, f32[2,64,7]{1,2,0:T(8,128)}, u32[]{:S(2)}) copy-start(f32[2,64,7]{1,2,0:T(8,128)} %get-tuple-element.125) | copy-start | bytes 10756
  162.0 2.5 %copy-start.5 = (f32[512,2,64,7]{0,2,3,1:T(8,128)S(1)}, f32[512,2,64,7]{0,2,3,1:T(8,128)}, u32[]{:S(2)}) copy-start(f32[512,2,64,7]{0,2,3,1:T(8,128)} %get-tuple-element.126) | copy-start | bytes 5505028
  162.0 2.5 %copy-start.27 = (pred[2,64,512]{2,1,0:T(8,128)(4,1)S(1)}, pred[2,64,512]{2,1,0:T(8,128)(4,1)}, u32[]{:S(2)}) copy-start(pred[2,64,512]{2,1,0:T(8,128)(4,1)} %copy-done.26) | copy-start | bytes 196612
  164.5 3.4 %copy-start.31 = (f32[2,64,7]{1,2,0:T(8,128)}, f32[2,64,7]{1,2,0:T(8,128)S(1)}, u32[]{:S(2)}) copy-start(f32[2,64,7]{1,2,0:T(8,128)S(1)} %max.53) | copy-start | bytes 10756
  169.5 4.8 %copy-start.4 = (f32[512,2,64,7]{0,2,3,1:T(8,128)S(1)}, f32[512,2,64,7]{0,2,3,1:T(8,128)}, u32[]{:S(2)}) copy-start(f32[512,2,64,7]{0,2,3,1:T(8,128)} %get-tuple-element.130) | copy-start | bytes 5505028
  169.5 4.8 %copy-start.25 = (pred[2,64,512]{2,1,0:T(8,128)(4,1)S(1)}, pred[2,64,512]{2,1,0:T(8,128)(4,1)}, u32[]{:S(2)}) copy-start(pred[2,64,512]{2,1,0:T(8,128)(4,1)} %copy-done.24) | copy-start | bytes 196612
  174.3 3.4 %copy-start.33 = (f32[2,64,7]{1,2,0:T(8,128)}, f32[2,64,7]{1,2,0:T(8,128)S(1)}, u32[]{:S(2)}) copy-start(f32[2,64,7]{1,2,0:T(8,128)S(1)} %max.52) | copy-start | bytes 10756
  178.4 3.8 %copy-start.3 = (f32[512,2,64,7]{0,2,3,1:T(8,128)S(1)}, f32[512,2,64,7]{0,2,3,1:T(8,128)}, u32[]{:S(2)}) copy-start(f32[512,2,64,7]{0,2,3,1:T(8,128)} %get-tuple-element.134) | copy-start | bytes 5505028
  178.5 3.8 %copy-start.23 = (pred[2,64,512]{2,1,0:T(8,128)(4,1)S(1)}, pred[2,64,512]{2,1,0:T(8,128)(4,1)}, u32[]{:S(2)}) copy-start(pred[2,64,512]{2,1,0:T(8,128)(4,1)} %copy-done.22) | copy-start | bytes 196612
  182.3 3.4 %copy-start.35 = (f32[2,64,7]{1,2,0:T(8,128)}, f32[2,64,7]{1,2,0:T(8,128)S(1)}, u32[]{:S(2)}) copy-start(f32[2,64,7]{1,2,0:T(8,128)S(1)} %max.51) | copy-start | bytes 10756
  184.5 2.0 %copy-start.8 = (bf16[2,64,1,7,128]{4,3,2,1,0:T(8,128)(2,1)S(1)}, bf16[2,64,1,7,128]{4,3,2,1,0:T(8,128)(2,1)}, u32[]{:S(2)}) copy-start(bf16[2,64,1,7,128]{4,3,2,1,0:T(8,128)(2,1)} %copy-done.7) | copy-start | bytes 688132
  184.5 2.1 %copy-start.16 = (pred[2,64,576]{2,1,0:T(8,128)(4,1)S(1)}, pred[2,64,576]{2,1,0:T(8,128)(4,1)}, u32[]{:S(2)}) copy-start(pred[2,64,576]{2,1,0:T(8,128)(4,1)} %get-tuple-element.83) | copy-start | bytes 221188
  186.4 0.8 copy-start.37
  186.4 1.5 copy-start.2
  186.4 1.5 copy-start.21
  187.9 2.1 %copy-start.19 = (pred[2,64,576]{2,1,0:T(8,128)(4,1)S(1)}, pred[2,64,576]{2,1,0:T(8,128)(4,1)}, u32[]{:S(2)}) copy-start(pred[2,64,576]{2,1,0:T(8,128)(4,1)} %get-tuple-element.86) | copy-start | bytes 221188
  187.9 2.1 %copy-start.32 = (f32[2,64,7]{1,2,0:T(8,128)S(1)}, f32[2,64,7]{1,2,0:T(8,128)}, u32[]{:S(2)}) copy-start(f32[2,64,7]{1,2,0:T(8,128)} %copy-done.31) | copy-start | bytes 10756
  189.4 1.7 copy-start
  189.4 1.6 copy-start.18
  189.4 1.6 copy-start.34
  190.0 1.9 copy-start.1
  190.1 1.9 copy-start.17
  190.1 1.9 copy-start.36
  192.0 1.7 copy-start.39
  192.0 1.8 copy-start.40
  192.0 1.8 copy-start.41
  192.9 1.0 copy-start.28
  192.9 1.1 copy-start.53
  194.0 1.0 copy-start.29
  194.0 1.1 copy-start.54
  195.2 1.0 copy-start.30
  195.2 1.1 copy-start.55
where the time goes:
time: 201 us; the launch traced here: 200 us
  blocking collectives  89.4 us (44%)
  local copies, waits for them, and re-layouts  42.6 us (21%)
  matrix products  27.8 us (14%)
  other arithmetic  24.3 us (12%)
  starting transfers between devices  15.2 us (8%)
    psum x1, blocking collectives, local(): lax.psum(contribution, ('head', 'inner', 'outer')).astype(jnp.bfloat16)  89.4 us
    ppermute x4, starting transfers between devices, shifted(): return lax.ppermute(block, axis, route)  15.2 us
    dot_general x4, matrix products, one_group(): jnp.einsum('qbrd,nd->qbrn', heads_here, vertical_pairs[g, :, :HD], prefer...  9.04 us
    dot_general x4, matrix products, one_group(): jnp.einsum('qbrn,nd->qbrd', vertical_weights.astype(jnp.bfloat16), vertic...  8.05 us
    dot_general x4, matrix products, one_group(): jnp.einsum('qbrd,qnd->qbrn', heads_here, slash_keys, preferred_element_ty...  8 us
    unnamed x118, local copies, waits for them, and re-layouts  7.7 us
    gather x1, local copies, waits for them, and re-layouts, owned_blocks(): gathered = flat_blocks[position]  5.7 us
    reduce_sum x4, other arithmetic, one_group(): jnp.sum(vertical_weights, axis=-1) + jnp.sum(slash_weights, axis=-1)  4.15 us
  transfers between devices with their start and end apart: 4, of which 0 were waited for; matrix products, arithmetic and copies ran while one was open for 25% of the time, Pallas kernels for 0%

commit v1 on v0

v1 whole, which is shorter than its diff:
```python
import math
import jax
import jax.numpy as jnp
import numpy as np
from jax import lax
from jax.experimental import pallas as pl
from jax.experimental.pallas import tpu as pltpu
from jax.sharding import Mesh, PartitionSpec as P

QH = 28
KVH = 4
HD = 128
BLOCK = 64
MAXV = 8
MAXS = 9
PER = QH // KVH
SIZES = (2, 2, 4, 4, 4)
AXES = ("zh", "c", "x", "y", "zl")
DEVICES = 256
CHUNK = 4
CAPACITY = 5 * CHUNK
NEGATIVE = -1e30
LOG2_SCALE = math.log2(math.e) * HD ** (-0.5)
VMEM = pl.BlockSpec(memory_space=pltpu.VMEM)
SMEM = pl.BlockSpec(memory_space=pltpu.SMEM)
ANY = pl.BlockSpec(memory_space=pl.ANY)


def owner_plane(block):
    return (block >> 3) & 31


def owner_layer(block):
    return ((block >> 8) << 2) | ((block >> 1) & 3)


def pack_kernel(key_ref, value_ref, packed_ref):
    for h in range(KVH):
        for kv, source in enumerate((key_ref, value_ref)):
            for quarter in range(4):
                for block in range(2):
                    packed_ref[h * 8 + kv * 4 + quarter, block * 16 : block * 16 + 16, :] = source[
                        block * 64 + quarter * 16 : block * 64 + quarter * 16 + 16,
                        h * HD : (h + 1) * HD,
                    ]


def pick_owned_kernel(place_ref, vertical_ref, received_ref, out_ref):
    head = place_ref[0] >> 3
    for j in range(MAXV):
        block = vertical_ref[head, j]
        piece = received_ref[owner_plane(block), block & 1]
        for copy in range(8):
            out_ref[copy, j] = piece


def pick_layer_kernel(place_ref, vertical_ref, received_ref, out_ref):
    head = place_ref[0] >> 3
    for j in range(MAXV):
        piece = received_ref[owner_layer(vertical_ref[head, j]), j]
        for copy in range(16):
            out_ref[copy, j] = piece


def attend_kernel(
    place_ref,
    vertical_ref,
    offsets_ref,
    counts_ref,
    query_ref,
    own_ref,
    second_ref,
    fourth_ref,
    odd_ref,
    near_ref,
    far_ref,
    out_ref,
    slab,
    pairs,
    keys,
    values,
    sems,
):
    step = pl.program_id(0)
    device = place_ref[1]
    half = step >> 1
    low = step & 1
    head = (((place_ref[0] >> 4) ^ half) << 1) | low

    @pl.when(step == 0)
    def _():
        copies = [
            pltpu.make_async_copy(fourth_ref, slab.at[0], sems.at[0]),
            pltpu.make_async_copy(odd_ref.at[1], slab.at[1], sems.at[1]),
            pltpu.make_async_copy(second_ref, slab.at[2], sems.at[2]),
            pltpu.make_async_copy(odd_ref.at[0], slab.at[3], sems.at[3]),
            pltpu.make_async_copy(own_ref, slab.at[4], sems.at[4]),
            pltpu.make_async_copy(near_ref, pairs.at[0], sems.at[5]),
            pltpu.make_async_copy(far_ref, pairs.at[1], sems.at[6]),
        ]
        for copy in copies:
            copy.start()
        keys[...] = jnp.zeros_like(keys)
        values[:, :HD] = jnp.zeros((CAPACITY * BLOCK, HD), jnp.bfloat16)
        values[:, HD:] = jnp.ones((CAPACITY * BLOCK, HD), jnp.bfloat16)
        for copy in copies:
            copy.wait()

    def put(slot, key, value):
        rows = pl.ds(pl.multiple_of(slot * BLOCK, BLOCK), BLOCK)
        keys[rows, :] = key.reshape(BLOCK, HD)
        values[rows, :HD] = value.reshape(BLOCK, HD)

    for local_block in range(2):
        block = device * 2 + local_block
        put(0, slab[4, head, 0, :, local_block], slab[4, head, 1, :, local_block])
        filled = jnp.int32(1)
        near = jnp.int32(0)
        for j in range(MAXV):
            vertical = vertical_ref[head, j]
            put(filled, pairs[half, low, 0, :, j], pairs[half, low, 1, :, j])
            live = (j < counts_ref[head, 0]) & (vertical < block)
            distance = block - vertical
            near = jnp.where(live & (distance <= 8), near | (1 << jnp.clip(distance, 0, 8)), near)
            filled = jnp.where(live, filled + 1, filled)
        for i in range(1, MAXS):
            offset = offsets_ref[head, i]
            live = (
                (i < counts_ref[head, 1]) & (block >= offset) & (((near >> offset) & 1) == 0)
            )
            place = local_block + 8 - offset
            put(
                filled,
                slab[place >> 1, head, 0, :, place & 1],
                slab[place >> 1, head, 1, :, place & 1],
            )
            filled = jnp.where(live, filled + 1, filled)

        rows = slice(local_block * BLOCK, (local_block + 1) * BLOCK)
        queries = jnp.concatenate(
            [query_ref[rows, r * HD : (r + 1) * HD] for r in range(PER)], axis=0
        )

        def run(chunks):
            width = CHUNK * BLOCK
            total = PER * BLOCK
            scores = []
            for chunk in range(chunks):
                part = lax.dot_general(
                    queries,
                    keys[chunk * width : (chunk + 1) * width, :],
                    (((1,), (1,)), ((), ())),
                    preferred_element_type=jnp.float32,
                )
                if chunk == 0 or chunk == chunks - 1:
                    lane = lax.broadcasted_iota(jnp.int32, (total, width), 1)
                    allowed = lane + chunk * width < filled * BLOCK
                    if chunk == 0:
                        token = lax.broadcasted_iota(jnp.int32, (total, width), 0) % BLOCK
                        allowed = allowed & ((lane >= BLOCK) | (lane <= token))
                    part = jnp.where(allowed, part, NEGATIVE)
                scores.append(part)
            highest = scores[0]
            for part in scores[1:]:
                highest = jnp.maximum(highest, part)
            highest = jnp.max(highest, axis=1, keepdims=True)
            weights = [
                jnp.exp2((part - highest) * LOG2_SCALE).astype(jnp.bfloat16) for part in scores
            ]
            weights = jnp.concatenate(weights, axis=1) if chunks > 1 else weights[0]
            attended = jnp.dot(
                weights, values[: chunks * width, :], preferred_element_type=jnp.float32
            )
            result = (attended[:, :HD] / attended[:, HD:]).astype(jnp.bfloat16)
            for r in range(PER):
                out_ref[rows, r * HD : (r + 1) * HD] = result[r * BLOCK : (r + 1) * BLOCK, :]

        for chunks in range(1, CAPACITY // CHUNK + 1):
            pl.when((filled + CHUNK - 1) // CHUNK == chunks)(lambda chunks=chunks: run(chunks))


def local(query, key, value, vertical_blocks, slash_offsets, block_counts):
    device = lax.axis_index(AXES)
    place = jnp.stack([lax.axis_index(("c", "x", "y")), device]).astype(jnp.int32)
    bf16 = jnp.bfloat16
    packed = pl.pallas_call(
        pack_kernel,
        out_shape=jax.ShapeDtypeStruct((32, 32, HD), bf16),
        in_specs=[VMEM, VMEM],
        out_specs=VMEM,
    )(key, value)

    def shifted(array, distance):
        route = [(i, i + distance) for i in range(DEVICES - distance)]
        return lax.ppermute(array, AXES, route)

    second = shifted(packed, 2)
    fourth = shifted(packed, 4)

    spread = lax.all_to_all(packed, ("c", "x", "y"), 0, 0, tiled=True)
    owned = pl.pallas_call(
        pick_owned_kernel,
        out_shape=jax.ShapeDtypeStruct((8, MAXV, 16, HD), bf16),
        in_specs=[SMEM, SMEM, VMEM],
        out_specs=VMEM,
    )(place, vertical_blocks, spread.reshape(32, 2, 16, HD))
    layers = lax.all_to_all(owned, ("zh", "zl"), 0, 0, tiled=True)
    pieces = pl.pallas_call(
        pick_layer_kernel,
        out_shape=jax.ShapeDtypeStruct((16, MAXV, 16, HD), bf16),
        in_specs=[SMEM, SMEM, VMEM],
        out_specs=VMEM,
    )(place, vertical_blocks, layers)
    near = lax.all_to_all(pieces, ("x", "y"), 0, 0, tiled=True)
    far = lax.ppermute(near, "c", [(0, 1), (1, 0)])

    odd = shifted(jnp.stack([packed, second]), 1)

    slab_shape = (KVH, 2, 4, 2, 16, HD)
    pair_shape = (2, 2, 4, MAXV, 16, HD)
    columns = pl.BlockSpec(
        (2 * BLOCK, PER * HD),
        lambda i, place_ref, *_: (0, (((place_ref[0] >> 4) ^ (i >> 1)) << 1) | (i & 1)),
    )
    return pl.pallas_call(
        attend_kernel,
        out_shape=jax.ShapeDtypeStruct((2 * BLOCK, QH * HD), bf16),
        grid_spec=pltpu.PrefetchScalarGridSpec(
            num_scalar_prefetch=4,
            grid=(KVH,),
            in_specs=[columns] + [ANY] * 6,
            out_specs=columns,
            scratch_shapes=[
                pltpu.VMEM((5,) + slab_shape, bf16),
                pltpu.VMEM((2,) + pair_shape, bf16),
                pltpu.VMEM((CAPACITY * BLOCK, HD), bf16),
                pltpu.VMEM((CAPACITY * BLOCK, 2 * HD), bf16),
                pltpu.SemaphoreType.DMA((7,)),
            ],
        ),
        compiler_params=pltpu.CompilerParams(vmem_limit_bytes=40 * 1024 * 1024),
        cost_estimate=pl.CostEstimate(
            flops=2_000_000_000, bytes_accessed=4_000_000, transcendentals=4_000_000
        ),
    )(
        place,
        vertical_blocks,
        slash_offsets,
        block_counts,
        query,
        packed.reshape(slab_shape),
        second.reshape(slab_shape),
        fourth.reshape(slab_shape),
        odd.reshape((2,) + slab_shape),
        near.reshape(pair_shape),
        far.reshape(pair_shape),
    )


def solution(mesh):
    finer = Mesh(np.asarray(mesh.devices).reshape(SIZES), AXES)
    return jax.shard_map(
        local,
        mesh=finer,
        in_specs=(P(AXES), P(AXES), P(AXES), P(), P(), P()),
        out_specs=P(AXES),
        check_vma=False,
    )
```

time: 201 us -> 102 us (0.51)
  the two profiles are of different devices: /device:TPU:1 before, /device:TPU:5 now
where the time goes in v1:
time: 102 us; the launch traced here: 100 us
  waiting for transfers between devices  42.6 us (42%)
  starting transfers between devices  21.4 us (21%)
  blocking collectives  18.4 us (18%)
  Pallas kernels  14.9 us (15%)
  other arithmetic  1.5 us (1%)
  local copies, waits for them, and re-layouts  1.47 us (1%)
    ppermute x3, waiting for transfers between devices, shifted(): return lax.ppermute(array, AXES, route)  36.5 us
    all_to_all x1, blocking collectives, local(): layers = lax.all_to_all(owned, ('zh', 'zl'), 0, 0, tiled=True)  18.4 us
    pallas_call x1, Pallas kernels, local(): pl.pallas_call(attend_kernel, out_shape=jax.ShapeDtypeStruct((2 * BLOCK,...  9.64 us
    all_to_all x1, starting transfers between devices, local(): spread = lax.all_to_all(packed, ('c', 'x', 'y'), 0, 0, tiled=True)  7.92 us
    all_to_all x1, waiting for transfers between devices, local(): spread = lax.all_to_all(packed, ('c', 'x', 'y'), 0, 0, tiled=True)  6.16 us
    all_to_all x1, starting transfers between devices, local(): near = lax.all_to_all(pieces, ('x', 'y'), 0, 0, tiled=True)  6.13 us
    ppermute x3, starting transfers between devices, shifted(): return lax.ppermute(array, AXES, route)  5.74 us
  transfers between devices with their start and end apart: 6, of which 3 were waited for; matrix products, arithmetic and copies ran while one was open for 2% of the time, Pallas kernels for 0%

profile of v1, /device:TPU:5, one launch (start us, length us, event | category | flops | bytes accessed | tf_op | source)
XLA Modules:
  0.0 100.5 jit_solution(13022910136389070159)
XLA Ops:
  0.0 1.7 %shard_map.64 = bf16[32,32,128]{2,1,0:T(8,128)(2,1)} custom-call(bf16[128,512]{1,0:T(8,128)(2,1)} %key_ref.1, bf16[128,512]{1,0:T(8,128)(2,1)} %value_ref.1), custom_call_target="tpu_custom_call" | custom-call | tf_op jit(solution)/shard_map/pallas_call | solution.py:186
  1.7 7.9 %all-to-all-start = ((bf16[32,32,128]{2,1,0:T(8,128)(2,1)}), bf16[32,32,128]{2,1,0:T(8,128)(2,1)S(1)}, u32[]{:S(2)}, u32[]{:S(2)}) async-start(bf16[32,32,128]{2,1,0:T(8,128)(2,1)} %shard_map.64), calls=%async_computation | async-start | bytes 524288 | tf_op jit(solution)/shard_map/all_to_all | solution.py:200
  9.7 0.7 pad_add_fusion.place_ref
  10.3 6.2 %all-to-all-done = bf16[32,32,128]{2,1,0:T(8,128)(2,1)S(1)} async-done(((bf16[32,32,128]{2,1,0:T(8,128)(2,1)}), bf16[32,32,128]{2,1,0:T(8,128)(2,1)S(1)}, u32[]{:S(2)}, u32[]{:S(2)}) %all-to-all-start) | async-done | bytes 262176 | tf_op jit(solution)/shard_map/all_to_all | solution.py:200
  16.5 0.0 copy-start.5
  16.5 0.7 copy-done.5
  17.2 1.7 %shard_map.65 = bf16[8,8,16,128]{3,2,1,0:T(8,128)(2,1)} custom-call(s32[2]{0:T(128)} %pad_add_fusion.place_ref, s32[4,8]{1,0:T(4,128)} %vertical_ref.5, bf16[32,2,16,128]{3,2,1,0:T(8,128)(2,1)} %bitcast.19), custom_call_target="tpu_custom_call" | custom-call | tf_op jit(solution)/shard_map/pallas_call | solution.py:201
  18.9 18.4 %all_to_all.15.received_ref = bf16[8,8,16,128]{3,2,1,0:T(8,128)(2,1)} all-to-all(bf16[8,8,16,128]{3,2,1,0:T(8,128)(2,1)} %shard_map.65), channel_id=1, replica_groups=mesh['zh'=2,'c'=2,'x'=4,'y'=4,'zl'=4] {'zh','zl'}, dimensions={0} | all-to-all | bytes 524288 | tf_op jit(solution)/shard_map/all_to_all | solution.py:207
  37.3 1.9 %shard_map.66 = bf16[16,8,16,128]{3,2,1,0:T(8,128)(2,1)} custom-call(s32[2]{0:T(128)} %pad_add_fusion.place_ref, s32[4,8]{1,0:T(4,128)} %vertical_ref.5, bf16[8,8,16,128]{3,2,1,0:T(8,128)(2,1)} %all_to_all.15.received_ref), custom_call_target="tpu_custom_call" | custom-call | tf_op jit(solution)/shard_map/pallas_call | solution.py:208
  39.1 0.0 copy-start
  39.1 0.0 copy-start.3
  39.1 6.1 %all-to-all-start.2 = ((bf16[16,8,16,128]{3,2,1,0:T(8,128)(2,1)}), bf16[16,8,16,128]{3,2,1,0:T(8,128)(2,1)S(1)}, u32[]{:S(2)}, u32[]{:S(2)}) async-start(bf16[16,8,16,128]{3,2,1,0:T(8,128)(2,1)} %shard_map.66), calls=%async_computation.2 | async-start | bytes 1048576 | tf_op jit(solution)/shard_map/all_to_all | solution.py:214
  45.3 0.0 copy-done
  45.3 1.9 %collective-permute-start = (bf16[32,32,128]{2,1,0:T(8,128)(2,1)S(1)}, bf16[32,32,128]{2,1,0:T(8,128)(2,1)S(1)}, u32[]{:S(2)}, u32[]{:S(2)}) collective-permute-start(bf16[32,32,128]{2,1,0:T(8,128)(2,1)S(1)} %copy-done), channel_id=1, source_target_pairs={{0,2},{1,3},{2,4},{3,5},{4,6},{5,7},{6,8},{7,9},{8,10},{9,11},{10,... | collective-permute-start | bytes 786440 | tf_op jit(solution)/shard_map/ppermute | solution.py:195
  47.2 15.7 %collective-permute-done = bf16[32,32,128]{2,1,0:T(8,128)(2,1)S(1)} collective-permute-done((bf16[32,32,128]{2,1,0:T(8,128)(2,1)S(1)}, bf16[32,32,128]{2,1,0:T(8,128)(2,1)S(1)}, u32[]{:S(2)}, u32[]{:S(2)}) %collective-permute-start) | collective-permute-done | bytes 262176 | tf_op jit(solution)/shard_map/ppermute | solution.py:195
  62.9 0.0 copy-start.6
  62.9 0.0 copy-start.4
  62.9 0.8 pad_maximum_fusion
  63.7 1.9 %collective-permute-start.2 = (bf16[2,32,32,128]{3,2,1,0:T(8,128)(2,1)}, bf16[2,32,32,128]{3,2,1,0:T(8,128)(2,1)S(1)}, u32[]{:S(2)}, u32[]{:S(2)}) collective-permute-start(bf16[2,32,32,128]{3,2,1,0:T(8,128)(2,1)} %pad_maximum_fusion), channel_id=1, source_target_pairs={{0,1},{1,2},{2,3},{3,4},{4,5},{5,6},{6,7},{7,8},{8,9},{9,10},{10,1... | collective-permute-start | bytes 1572872 | tf_op jit(solution)/shard_map/ppermute | solution.py:195
  65.6 0.0 all-to-all-done.2
  65.6 1.7 %collective-permute-start.3 = (bf16[16,8,16,128]{3,2,1,0:T(8,128)(2,1)S(1)}, bf16[16,8,16,128]{3,2,1,0:T(8,128)(2,1)S(1)}, u32[]{:S(2)}, u32[]{:S(2)}) collective-permute-start(bf16[16,8,16,128]{3,2,1,0:T(8,128)(2,1)S(1)} %all-to-all-done.2), channel_id=1, source_target_pairs={{0,64},{64,0},{1,65},{65,1},{2,66},{66,2},{3,67},{67,3},{4,68},{68... | collective-permute-start | bytes 1572872 | tf_op jit(solution)/shard_map/ppermute | solution.py:215
  67.3 1.9 %collective-permute-start.1 = (bf16[32,32,128]{2,1,0:T(8,128)(2,1)S(1)}, bf16[32,32,128]{2,1,0:T(8,128)(2,1)S(1)}, u32[]{:S(2)}, u32[]{:S(2)}) collective-permute-start(bf16[32,32,128]{2,1,0:T(8,128)(2,1)S(1)} %copy-done), channel_id=1, source_target_pairs={{0,4},{1,5},{2,6},{3,7},{4,8},{5,9},{6,10},{7,11},{8,12},{9,13},{1... | collective-permute-start | bytes 786440 | tf_op jit(solution)/shard_map/ppermute | solution.py:195
  69.2 0.0 copy-done.6
  69.2 0.1 copy.7.counts_ref
  69.3 20.8 %collective-permute-done.1 = bf16[32,32,128]{2,1,0:T(8,128)(2,1)S(1)} collective-permute-done((bf16[32,32,128]{2,1,0:T(8,128)(2,1)S(1)}, bf16[32,32,128]{2,1,0:T(8,128)(2,1)S(1)}, u32[]{:S(2)}, u32[]{:S(2)}) %collective-permute-start.1) | collective-permute-done | bytes 262176 | tf_op jit(solution)/shard_map/ppermute | solution.py:195
  90.1 0.0 collective-permute-done.2
  90.1 0.0 collective-permute-done.3
  90.1 0.0 copy-start.1
  90.1 0.0 copy-start.2
  90.2 0.0 copy-done.3
  90.2 0.0 copy-done.4
  90.2 0.6 copy-done.1
  90.8 0.0 copy-done.2
  90.8 9.6 %shard_map.67 = bf16[128,3584]{1,0:T(8,128)(2,1)} custom-call(s32[2]{0:T(128)S(1)} %copy-done.2, s32[4,8]{1,0:T(4,128)S(1)} %copy-done.1, s32[4,9]{1,0:T(4,128)S(1)} %copy-done.4, s32[4,2]{1,0:T(4,128)S(1)} %copy.7.counts_ref, bf16[128,3584]{1,0:T(8,128)(2,1)S(1)} %copy-done.3, bf16[4,2,4,2,16,128]{5,4,3,2,1,0:T(8,128)(2,1)S(1)} %bitcast.12, ...), custom_call_target="tpu_custom_call" | custom-call | flops 2000000000 | bytes 4000000 | tf_op jit(solution)/shard_map/pallas_call | solution.py:225
Async XLA Ops:
  1.7 14.8 %all-to-all-start = ((bf16[32,32,128]{2,1,0:T(8,128)(2,1)}), bf16[32,32,128]{2,1,0:T(8,128)(2,1)S(1)}, u32[]{:S(2)}, u32[]{:S(2)}) async-start(bf16[32,32,128]{2,1,0:T(8,128)(2,1)} %shard_map.64), calls=%async_computation | async-start | bytes 524288 | tf_op jit(solution)/shard_map/all_to_all | solution.py:200
  16.5 0.7 copy-start.5
  39.1 6.1 %copy-start = (bf16[32,32,128]{2,1,0:T(8,128)(2,1)S(1)}, bf16[32,32,128]{2,1,0:T(8,128)(2,1)}, u32[]{:S(2)}) copy-start(bf16[32,32,128]{2,1,0:T(8,128)(2,1)} %shard_map.64) | copy-start | bytes 786436
  39.1 51.0 %copy-start.3 = (bf16[128,3584]{1,0:T(8,128)(2,1)S(1)}, bf16[128,3584]{1,0:T(8,128)(2,1)}, u32[]{:S(2)}) copy-start(bf16[128,3584]{1,0:T(8,128)(2,1)} %query_ref.1) | copy-start | bytes 2752516
  39.1 26.5 %all-to-all-start.2 = ((bf16[16,8,16,128]{3,2,1,0:T(8,128)(2,1)}), bf16[16,8,16,128]{3,2,1,0:T(8,128)(2,1)S(1)}, u32[]{:S(2)}, u32[]{:S(2)}) async-start(bf16[16,8,16,128]{3,2,1,0:T(8,128)(2,1)} %shard_map.66), calls=%async_computation.2 | async-start | bytes 1048576 | tf_op jit(solution)/shard_map/all_to_all | solution.py:214
  45.3 17.6 %collective-permute-start = (bf16[32,32,128]{2,1,0:T(8,128)(2,1)S(1)}, bf16[32,32,128]{2,1,0:T(8,128)(2,1)S(1)}, u32[]{:S(2)}, u32[]{:S(2)}) collective-permute-start(bf16[32,32,128]{2,1,0:T(8,128)(2,1)S(1)} %copy-done), channel_id=1, source_target_pairs={{0,2},{1,3},{2,4},{3,5},{4,6},{5,7},{6,8},{7,9},{8,10},{9,11},{10,... | collective-permute-start | bytes 786440 | tf_op jit(solution)/shard_map/ppermute | solution.py:195
  62.9 6.4 %copy-start.6 = (s32[4,2]{0,1:T(2,128)S(1)}, s32[4,2]{0,1:T(2,128)}, u32[]{:S(2)}) copy-start(s32[4,2]{0,1:T(2,128)} %param.11) | copy-start | bytes 100
  62.9 27.3 %copy-start.4 = (s32[4,9]{1,0:T(4,128)S(1)}, s32[4,9]{1,0:T(4,128)}, u32[]{:S(2)}) copy-start(s32[4,9]{1,0:T(4,128)} %offsets_ref.1) | copy-start | bytes 436
  63.7 26.4 %collective-permute-start.2 = (bf16[2,32,32,128]{3,2,1,0:T(8,128)(2,1)}, bf16[2,32,32,128]{3,2,1,0:T(8,128)(2,1)S(1)}, u32[]{:S(2)}, u32[]{:S(2)}) collective-permute-start(bf16[2,32,32,128]{3,2,1,0:T(8,128)(2,1)} %pad_maximum_fusion), channel_id=1, source_target_pairs={{0,1},{1,2},{2,3},{3,4},{4,5},{5,6},{6,7},{7,8},{8,9},{9,10},{10,1... | collective-permute-start | bytes 1572872 | tf_op jit(solution)/shard_map/ppermute | solution.py:195
  65.6 24.5 %collective-permute-start.3 = (bf16[16,8,16,128]{3,2,1,0:T(8,128)(2,1)S(1)}, bf16[16,8,16,128]{3,2,1,0:T(8,128)(2,1)S(1)}, u32[]{:S(2)}, u32[]{:S(2)}) collective-permute-start(bf16[16,8,16,128]{3,2,1,0:T(8,128)(2,1)S(1)} %all-to-all-done.2), channel_id=1, source_target_pairs={{0,64},{64,0},{1,65},{65,1},{2,66},{66,2},{3,67},{67,3},{4,68},{68... | collective-permute-start | bytes 1572872 | tf_op jit(solution)/shard_map/ppermute | solution.py:215
  67.3 22.8 %collective-permute-start.1 = (bf16[32,32,128]{2,1,0:T(8,128)(2,1)S(1)}, bf16[32,32,128]{2,1,0:T(8,128)(2,1)S(1)}, u32[]{:S(2)}, u32[]{:S(2)}) collective-permute-start(bf16[32,32,128]{2,1,0:T(8,128)(2,1)S(1)} %copy-done), channel_id=1, source_target_pairs={{0,4},{1,5},{2,6},{3,7},{4,8},{5,9},{6,10},{7,11},{8,12},{9,13},{1... | collective-permute-start | bytes 786440 | tf_op jit(solution)/shard_map/ppermute | solution.py:195
  90.1 0.7 copy-start.1
  90.1 0.7 copy-start.2

commit v2 on v1

--- a/solution.py
+++ b/solution.py
@@ -24,6 +24,7 @@
 VMEM = pl.BlockSpec(memory_space=pltpu.VMEM)
 SMEM = pl.BlockSpec(memory_space=pltpu.SMEM)
 ANY = pl.BlockSpec(memory_space=pl.ANY)
+THREE_BACK = [(0, 3), (1, 0), (2, 1), (3, 2)]
 
 
 def owner_plane(block):
@@ -34,27 +35,40 @@
     return ((block >> 8) << 2) | ((block >> 1) & 3)
 
 
-def pack_kernel(key_ref, value_ref, packed_ref):
+def pack_kernel(key_ref, value_ref, packed_ref, slab_ref):
     for h in range(KVH):
         for kv, source in enumerate((key_ref, value_ref)):
-            for quarter in range(4):
-                for block in range(2):
-                    packed_ref[h * 8 + kv * 4 + quarter, block * 16 : block * 16 + 16, :] = source[
-                        block * 64 + quarter * 16 : block * 64 + quarter * 16 + 16,
-                        h * HD : (h + 1) * HD,
+            for block in range(2):
+                tokens = source[block * BLOCK : (block + 1) * BLOCK, h * HD : (h + 1) * HD]
+                slab_ref[h, kv, block] = tokens
+                for quarter in range(4):
+                    packed_ref[h * 8 + kv * 4 + quarter, block * 16 : block * 16 + 16, :] = tokens[
+                        quarter * 16 : quarter * 16 + 16
                     ]
 
 
-def pick_owned_kernel(place_ref, vertical_ref, received_ref, out_ref):
+def pick_owned_kernel(
+    place_ref, vertical_ref, received_ref, own_ref, fourth_ref, first_ref, out_ref, chosen_ref
+):
     head = place_ref[0] >> 3
     for j in range(MAXV):
         block = vertical_ref[head, j]
         piece = received_ref[owner_plane(block), block & 1]
         for copy in range(8):
             out_ref[copy, j] = piece
-
-
-def pick_layer_kernel(place_ref, vertical_ref, received_ref, out_ref):
+    first_of_line = (place_ref[1] & 3) == 0
+
+    @pl.when(first_of_line)
+    def _():
+        chosen_ref[...] = own_ref[...]
+
+    @pl.when(jnp.logical_not(first_of_line))
+    def _():
+        chosen_ref[...] = fourth_ref[...]
+
+
+def pick_layer_kernel(place_ref, vertical_ref, received_ref, chosen_ref, first_ref, *refs):
+    out_ref = refs[-3]
     head = place_ref[0] >> 3
     for j in range(MAXV):
         piece = received_ref[owner_layer(vertical_ref[head, j]), j]
@@ -69,9 +83,10 @@
     counts_ref,
     query_ref,
     own_ref,
+    fourth_ref,
+    third_ref,
     second_ref,
-    fourth_ref,
-    odd_ref,
+    first_ref,
     near_ref,
     far_ref,
     out_ref,
@@ -81,22 +96,20 @@
     values,
     sems,
 ):
-    step = pl.program_id(0)
+    head = pl.program_id(0)
     device = place_ref[1]
-    half = step >> 1
-    low = step & 1
-    head = (((place_ref[0] >> 4) ^ half) << 1) | low
-
-    @pl.when(step == 0)
+
+    @pl.when(head == 0)
     def _():
+        mine = (place_ref[0] >> 4) * 2
         copies = [
             pltpu.make_async_copy(fourth_ref, slab.at[0], sems.at[0]),
-            pltpu.make_async_copy(odd_ref.at[1], slab.at[1], sems.at[1]),
+            pltpu.make_async_copy(third_ref, slab.at[1], sems.at[1]),
             pltpu.make_async_copy(second_ref, slab.at[2], sems.at[2]),
-            pltpu.make_async_copy(odd_ref.at[0], slab.at[3], sems.at[3]),
+            pltpu.make_async_copy(first_ref, slab.at[3], sems.at[3]),
             pltpu.make_async_copy(own_ref, slab.at[4], sems.at[4]),
-            pltpu.make_async_copy(near_ref, pairs.at[0], sems.at[5]),
-            pltpu.make_async_copy(far_ref, pairs.at[1], sems.at[6]),
+            pltpu.make_async_copy(near_ref, pairs.at[pl.ds(mine, 2)], sems.at[5]),
+            pltpu.make_async_copy(far_ref, pairs.at[pl.ds(2 - mine, 2)], sems.at[6]),
         ]
         for copy in copies:
             copy.start()
@@ -113,12 +126,12 @@
 
     for local_block in range(2):
         block = device * 2 + local_block
-        put(0, slab[4, head, 0, :, local_block], slab[4, head, 1, :, local_block])
+        put(0, slab[4, head, 0, local_block], slab[4, head, 1, local_block])
         filled = jnp.int32(1)
         near = jnp.int32(0)
         for j in range(MAXV):
             vertical = vertical_ref[head, j]
-            put(filled, pairs[half, low, 0, :, j], pairs[half, low, 1, :, j])
+            put(filled, pairs[head, 0, :, j], pairs[head, 1, :, j])
             live = (j < counts_ref[head, 0]) & (vertical < block)
             distance = block - vertical
             near = jnp.where(live & (distance <= 8), near | (1 << jnp.clip(distance, 0, 8)), near)
@@ -131,8 +144,8 @@
             place = local_block + 8 - offset
             put(
                 filled,
-                slab[place >> 1, head, 0, :, place & 1],
-                slab[place >> 1, head, 1, :, place & 1],
+                slab[place >> 1, head, 0, place & 1],
+                slab[place >> 1, head, 1, place & 1],
             )
             filled = jnp.where(live, filled + 1, filled)
 
@@ -179,48 +192,81 @@
             pl.when((filled + CHUNK - 1) // CHUNK == chunks)(lambda chunks=chunks: run(chunks))
 
 
+def hand_on_kernel(*refs):
+    pass
+
+
+def hold(*arrays):
+    count = len(arrays)
+    return pl.pallas_call(
+        hand_on_kernel,
+        out_shape=tuple(jax.ShapeDtypeStruct(array.shape, array.dtype) for array in arrays),
+        in_specs=[ANY] * count,
+        out_specs=(ANY,) * count,
+        input_output_aliases={i: i for i in range(count)},
+        cost_estimate=pl.CostEstimate(
+            flops=40_000_000_000, bytes_accessed=1_000_000, transcendentals=0
+        ),
+    )(*arrays)
+
+
+def after(array, *others):
+    return pl.pallas_call(
+        hand_on_kernel,
+        out_shape=jax.ShapeDtypeStruct(array.shape, array.dtype),
+        in_specs=[ANY] * (1 + len(others)),
+        out_specs=ANY,
+        input_output_aliases={0: 0},
+    )(array, *others)
+
+
 def local(query, key, value, vertical_blocks, slash_offsets, block_counts):
     device = lax.axis_index(AXES)
-    place = jnp.stack([lax.axis_index(("c", "x", "y")), device]).astype(jnp.int32)
+    place = jnp.stack([lax.axis_index(("c", "x", "y")), device, lax.axis_index(("zh", "zl"))]).astype(jnp.int32)
     bf16 = jnp.bfloat16
-    packed = pl.pallas_call(
+    slab_shape = jax.ShapeDtypeStruct((KVH, 2, 2, BLOCK, HD), bf16)
+    packed, own = pl.pallas_call(
         pack_kernel,
-        out_shape=jax.ShapeDtypeStruct((32, 32, HD), bf16),
+        out_shape=(jax.ShapeDtypeStruct((32, 32, HD), bf16), slab_shape),
         in_specs=[VMEM, VMEM],
-        out_specs=VMEM,
+        out_specs=(VMEM, VMEM),
     )(key, value)
 
     def shifted(array, distance):
         route = [(i, i + distance) for i in range(DEVICES - distance)]
         return lax.ppermute(array, AXES, route)
 
-    second = shifted(packed, 2)
-    fourth = shifted(packed, 4)
-
+    fourth = shifted(own, 4)
+    first = shifted(own, 1)
     spread = lax.all_to_all(packed, ("c", "x", "y"), 0, 0, tiled=True)
-    owned = pl.pallas_call(
+    owned, chosen = pl.pallas_call(
         pick_owned_kernel,
-        out_shape=jax.ShapeDtypeStruct((8, MAXV, 16, HD), bf16),
-        in_specs=[SMEM, SMEM, VMEM],
-        out_specs=VMEM,
-    )(place, vertical_blocks, spread.reshape(32, 2, 16, HD))
+        out_shape=(jax.ShapeDtypeStruct((8, MAXV, 16, HD), bf16), slab_shape),
+        in_specs=[SMEM, SMEM, VMEM, VMEM, VMEM, VMEM],
+        out_specs=(VMEM, VMEM),
+    )(place, vertical_blocks, spread.reshape(32, 2, 16, HD), own, fourth, first)
     layers = lax.all_to_all(owned, ("zh", "zl"), 0, 0, tiled=True)
-    pieces = pl.pallas_call(
+    late = [
+    ]
+    pieces, chosen, first = pl.pallas_call(
         pick_layer_kernel,
-        out_shape=jax.ShapeDtypeStruct((16, MAXV, 16, HD), bf16),
-        in_specs=[SMEM, SMEM, VMEM],
-        out_specs=VMEM,
-    )(place, vertical_blocks, layers)
+        out_shape=(jax.ShapeDtypeStruct((16, MAXV, 16, HD), bf16), slab_shape, slab_shape),
+        in_specs=[SMEM, SMEM, VMEM, ANY, ANY] + [ANY] * len(late),
+        out_specs=(VMEM, ANY, ANY),
+        input_output_aliases={3: 1, 4: 2},
+    )(place, vertical_blocks, layers, chosen, first, *late)
+    third = lax.ppermute(chosen, "zl", THREE_BACK)
+    second = shifted(first, 1)
     near = lax.all_to_all(pieces, ("x", "y"), 0, 0, tiled=True)
+    third, second = hold(third, second)
+    near = after(near, third, second)
     far = lax.ppermute(near, "c", [(0, 1), (1, 0)])
 
-    odd = shifted(jnp.stack([packed, second]), 1)
-
-    slab_shape = (KVH, 2, 4, 2, 16, HD)
-    pair_shape = (2, 2, 4, MAXV, 16, HD)
+    pair_shape = (KVH, 2, 4, MAXV, 16, HD)
+    half_shape = (KVH // 2, 2, 4, MAXV, 16, HD)
     columns = pl.BlockSpec(
         (2 * BLOCK, PER * HD),
-        lambda i, place_ref, *_: (0, (((place_ref[0] >> 4) ^ (i >> 1)) << 1) | (i & 1)),
+        lambda i, *_: (0, i),
     )
     return pl.pallas_call(
         attend_kernel,
@@ -228,11 +274,11 @@
         grid_spec=pltpu.PrefetchScalarGridSpec(
             num_scalar_prefetch=4,
             grid=(KVH,),
-            in_specs=[columns] + [ANY] * 6,
+            in_specs=[columns] + [ANY] * 7,
             out_specs=columns,
             scratch_shapes=[
-                pltpu.VMEM((5,) + slab_shape, bf16),
-                pltpu.VMEM((2,) + pair_shape, bf16),
+                pltpu.VMEM((5,) + slab_shape.shape, bf16),
+                pltpu.VMEM(pair_shape, bf16),
                 pltpu.VMEM((CAPACITY * BLOCK, HD), bf16),
                 pltpu.VMEM((CAPACITY * BLOCK, 2 * HD), bf16),
                 pltpu.SemaphoreType.DMA((7,)),
@@ -248,12 +294,13 @@
         slash_offsets,
         block_counts,
         query,
-        packed.reshape(slab_shape),
-        second.reshape(slab_shape),
-        fourth.reshape(slab_shape),
-        odd.reshape((2,) + slab_shape),
-        near.reshape(pair_shape),
-        far.reshape(pair_shape),
+        own,
+        fourth,
+        third,
+        second,
+        first,
+        near.reshape(half_shape),
+        far.reshape(half_shape),
     )
 
 

time: 102 us -> 87.5 us (0.86)
  the two profiles are of different devices: /device:TPU:5 before, /device:TPU:1 now
where the time goes in v2:
time: 87.5 us; the launch traced here: 86.9 us
  starting transfers between devices  28.6 us (33%)
  waiting for transfers between devices  20.8 us (24%)
  blocking collectives  17.2 us (20%)
  Pallas kernels  15.4 us (18%)
  local copies, waits for them, and re-layouts  4.13 us (5%)
    all_to_all x1, blocking collectives, local(): layers = lax.all_to_all(owned, ('zh', 'zl'), 0, 0, tiled=True)  17.2 us
    all_to_all x1, starting transfers between devices, local(): spread = lax.all_to_all(packed, ('c', 'x', 'y'), 0, 0, tiled=True)  11.9 us
    ppermute x3, starting transfers between devices, shifted(): return lax.ppermute(array, AXES, route)  10.3 us
    pallas_call x1, Pallas kernels, local(): pl.pallas_call(attend_kernel, out_shape=jax.ShapeDtypeStruct((2 * BLOCK,...  9.61 us
    ppermute x3, waiting for transfers between devices, shifted(): return lax.ppermute(array, AXES, route)  8.69 us
    all_to_all x1, waiting for transfers between devices, local(): spread = lax.all_to_all(packed, ('c', 'x', 'y'), 0, 0, tiled=True)  8.14 us
    unnamed x35, local copies, waits for them, and re-layouts  4.13 us
    all_to_all x1, starting transfers between devices, local(): near = lax.all_to_all(pieces, ('x', 'y'), 0, 0, tiled=True)  3.59 us
  transfers between devices with their start and end apart: 7, of which 4 were waited for; matrix products, arithmetic and copies ran while one was open for 1% of the time, Pallas kernels for 0%

profile of v2, /device:TPU:1, one launch (start us, length us, event | category | flops | bytes accessed | tf_op | source)
XLA Modules:
  0.0 86.9 jit_solution(6474771589781230806)
XLA Ops:
  0.0 1.8 %shard_map.64 = (bf16[32,32,128]{2,1,0:T(8,128)(2,1)}, bf16[4,2,2,64,128]{4,3,2,1,0:T(8,128)(2,1)}) custom-call(bf16[128,512]{1,0:T(8,128)(2,1)} %key_ref.1, bf16[128,512]{1,0:T(8,128)(2,1)} %value_ref.1), custom_call_target="tpu_custom_call" | custom-call | tf_op jit(solution)/shard_map/pallas_call | solution.py:228
  1.8 4.4 %collective-permute-start.1 = (bf16[4,2,2,64,128]{4,3,2,1,0:T(8,128)(2,1)}, bf16[4,2,2,64,128]{4,3,2,1,0:T(8,128)(2,1)S(1)}, u32[]{:S(2)}, u32[]{:S(2)}) collective-permute-start(bf16[4,2,2,64,128]{4,3,2,1,0:T(8,128)(2,1)} %get-tuple-element.14.own_ref), channel_id=1, source_target_pairs={{0,1},{1,2},{2,3},{3,4},{4,5},{5,6},{6,7},{7,8},{8,9},{9,10},{10,1... | collective-permute-start | bytes 786440 | tf_op jit(solution)/shard_map/ppermute | solution.py:237
  6.2 3.2 %collective-permute-start = (bf16[4,2,2,64,128]{4,3,2,1,0:T(8,128)(2,1)}, bf16[4,2,2,64,128]{4,3,2,1,0:T(8,128)(2,1)S(1)}, u32[]{:S(2)}, u32[]{:S(2)}) collective-permute-start(bf16[4,2,2,64,128]{4,3,2,1,0:T(8,128)(2,1)} %get-tuple-element.14.own_ref), channel_id=1, source_target_pairs={{0,4},{1,5},{2,6},{3,7},{4,8},{5,9},{6,10},{7,11},{8,12},{9,13},{1... | collective-permute-start | bytes 786440 | tf_op jit(solution)/shard_map/ppermute | solution.py:237
  9.4 11.9 %all-to-all-start = ((bf16[32,32,128]{2,1,0:T(8,128)(2,1)}), bf16[32,32,128]{2,1,0:T(8,128)(2,1)S(1)}, u32[]{:S(2)}, u32[]{:S(2)}) async-start(bf16[32,32,128]{2,1,0:T(8,128)(2,1)} %get-tuple-element.15), calls=%async_computation | async-start | bytes 524288 | tf_op jit(solution)/shard_map/all_to_all | solution.py:241
  21.3 0.7 pad_add_fusion.place_ref
  22.0 8.1 %all-to-all-done = bf16[32,32,128]{2,1,0:T(8,128)(2,1)S(1)} async-done(((bf16[32,32,128]{2,1,0:T(8,128)(2,1)}), bf16[32,32,128]{2,1,0:T(8,128)(2,1)S(1)}, u32[]{:S(2)}, u32[]{:S(2)}) %all-to-all-start) | async-done | bytes 262176 | tf_op jit(solution)/shard_map/all_to_all | solution.py:241
  30.1 0.0 copy-start.15
  30.1 0.0 collective-permute-done.1.first_ref
  30.1 0.0 copy-start.2
  30.1 0.0 collective-permute-done.fourth_ref
  30.1 0.0 copy-start.5
  30.2 0.7 copy-done.15
  30.8 0.1 copy-done.2
  30.9 0.1 copy-done.5
  31.0 2.1 %shard_map.65 = (bf16[8,8,16,128]{3,2,1,0:T(8,128)(2,1)}, bf16[4,2,2,64,128]{4,3,2,1,0:T(8,128)(2,1)}) custom-call(s32[3]{0:T(128)} %pad_add_fusion.place_ref, s32[4,8]{1,0:T(4,128)} %vertical_ref.5, bf16[32,2,16,128]{3,2,1,0:T(8,128)(2,1)} %bitcast.8, bf16[4,2,2,64,128]{4,3,2,1,0:T(8,128)(2,1)} %get-tuple-element.14.own_ref, ...), custom_call_target="tpu_custom_call" | custom-call | tf_op jit(solution)/shard_map/pallas_call | solution.py:242
  33.1 17.2 %all_to_all.15.received_ref = bf16[8,8,16,128]{3,2,1,0:T(8,128)(2,1)} all-to-all(bf16[8,8,16,128]{3,2,1,0:T(8,128)(2,1)} %get-tuple-element.16), channel_id=1, replica_groups=mesh['zh'=2,'c'=2,'x'=4,'y'=4,'zl'=4] {'zh','zl'}, dimensions={0} | all-to-all | bytes 524288 | tf_op jit(solution)/shard_map/all_to_all | solution.py:248
  50.3 1.9 %shard_map.66 = (bf16[16,8,16,128]{3,2,1,0:T(8,128)(2,1)}, bf16[4,2,2,64,128]{4,3,2,1,0:T(8,128)(2,1)}, bf16[4,2,2,64,128]{4,3,2,1,0:T(8,128)(2,1)}) custom-call(s32[3]{0:T(128)} %pad_add_fusion.place_ref, s32[4,8]{1,0:T(4,128)} %vertical_ref.5, bf16[8,8,16,128]{3,2,1,0:T(8,128)(2,1)} %all_to_all.15.received_ref, ...), custom_call_target="tpu_custom_call", output_to_operand_aliasing={{1}: (3, {}), {2}: (4, {})} | custom-call | tf_op jit(solution)/shard_map/pallas_call | solution.py:251
  52.2 0.6 collective-permute-start.2
  52.8 2.8 %collective-permute-start.3 = (bf16[4,2,2,64,128]{4,3,2,1,0:T(8,128)(2,1)}, bf16[4,2,2,64,128]{4,3,2,1,0:T(8,128)(2,1)S(1)}, u32[]{:S(2)}, u32[]{:S(2)}) collective-permute-start(bf16[4,2,2,64,128]{4,3,2,1,0:T(8,128)(2,1)} %get-tuple-element.19.first_ref), channel_id=1, source_target_pairs={{0,1},{1,2},{2,3},{3,4},{4,5},{5,6},{6,7},{7,8},{8,9},{9,10},{10,1... | collective-permute-start | bytes 786440 | tf_op jit(solution)/shard_map/ppermute | solution.py:237
  55.5 3.6 %all-to-all-start.2 = ((bf16[16,8,16,128]{3,2,1,0:T(8,128)(2,1)}), bf16[16,8,16,128]{3,2,1,0:T(8,128)(2,1)S(1)}, u32[]{:S(2)}, u32[]{:S(2)}) async-start(bf16[16,8,16,128]{3,2,1,0:T(8,128)(2,1)} %get-tuple-element.22), calls=%async_computation.2 | async-start | bytes 1048576 | tf_op jit(solution)/shard_map/all_to_all | solution.py:260
  59.1 0.0 collective-permute-done.2.refs_0_
  59.1 0.0 copy-start.7
  59.2 8.7 %collective-permute-done.3.refs_1_ = bf16[4,2,2,64,128]{4,3,2,1,0:T(8,128)(2,1)S(1)} collective-permute-done((bf16[4,2,2,64,128]{4,3,2,1,0:T(8,128)(2,1)}, bf16[4,2,2,64,128]{4,3,2,1,0:T(8,128)(2,1)S(1)}, u32[]{:S(2)}, u32[]{:S(2)}) %collective-permute-start.3) | collective-permute-done | bytes 262176 | tf_op jit(solution)/shard_map/ppermute | solution.py:237
  67.8 0.0 copy-done.7
  67.8 0.0 copy-start.9
  67.9 0.7 copy-done.9
  68.5 0.0 copy-start.13
  68.5 2.3 %all-to-all-done.2.refs_0_ = bf16[16,8,16,128]{3,2,1,0:T(8,128)(2,1)S(1)} async-done(((bf16[16,8,16,128]{3,2,1,0:T(8,128)(2,1)}), bf16[16,8,16,128]{3,2,1,0:T(8,128)(2,1)S(1)}, u32[]{:S(2)}, u32[]{:S(2)}) %all-to-all-start.2) | async-done | bytes 524320 | tf_op jit(solution)/shard_map/all_to_all | solution.py:260
  70.8 0.0 copy-start
  70.8 0.8 copy-done
  71.6 0.0 copy-start.16
  71.6 0.0 copy-start.3
  71.6 0.0 copy-start.4
  71.6 0.0 copy-start.6
  71.6 0.0 copy-start.8
  71.7 0.0 copy-start.10
  71.7 2.2 %collective-permute-start.4 = (bf16[16,8,16,128]{3,2,1,0:T(8,128)(2,1)}, bf16[16,8,16,128]{3,2,1,0:T(8,128)(2,1)S(1)}, u32[]{:S(2)}, u32[]{:S(2)}) collective-permute-start(bf16[16,8,16,128]{3,2,1,0:T(8,128)(2,1)} %shard_map.68), channel_id=1, source_target_pairs={{0,64},{64,0},{1,65},{65,1},{2,66},{66,2},{3,67},{67,3},{4,68},{68... | collective-permute-start | bytes 1572872 | tf_op jit(solution)/shard_map/ppermute | solution.py:263
  73.9 0.0 copy-done.16
  73.9 0.0 copy-start.14
  73.9 0.1 copy.12.counts_ref
  74.0 0.0 copy-start.11
  74.0 1.6 %collective-permute-done.4 = bf16[16,8,16,128]{3,2,1,0:T(8,128)(2,1)S(1)} collective-permute-done((bf16[16,8,16,128]{3,2,1,0:T(8,128)(2,1)}, bf16[16,8,16,128]{3,2,1,0:T(8,128)(2,1)S(1)}, u32[]{:S(2)}, u32[]{:S(2)}) %collective-permute-start.4) | collective-permute-done | bytes 524320 | tf_op jit(solution)/shard_map/ppermute | solution.py:263
  75.6 0.0 copy-start.12
  75.6 0.0 copy-done.13
  75.6 0.0 copy-done.3
  75.6 0.0 copy-done.4
  75.6 0.0 copy-done.6
  75.6 0.0 copy-done.8
  75.6 0.0 copy-done.10
  75.7 0.0 copy-done.14
  75.7 0.0 copy-done.11
  75.7 0.6 copy-done.12
  76.3 0.0 copy-start.1
  76.3 1.0 %copy-done.1 = bf16[16,8,16,128]{3,2,1,0:T(8,128)(2,1)S(1)} copy-done((bf16[16,8,16,128]{3,2,1,0:T(8,128)(2,1)S(1)}, bf16[16,8,16,128]{3,2,1,0:T(8,128)(2,1)}, u32[]{:S(2)}) %copy-start.1) | copy-done | bytes 524312
  77.3 9.6 %shard_map.69 = bf16[128,3584]{1,0:T(8,128)(2,1)} custom-call(s32[3]{0:T(128)S(1)} %copy-done.12, s32[4,8]{1,0:T(4,128)S(1)} %copy-done.11, s32[4,9]{1,0:T(4,128)S(1)} %copy-done.14, s32[4,2]{1,0:T(4,128)S(1)} %copy.12.counts_ref, bf16[128,3584]{1,0:T(8,128)(2,1)S(1)} %copy-done.13, bf16[4,2,2,64,128]{4,3,2,1,0:T(8,128)(2,1)S(1)} %copy-done.4, ...), custom_call_target="tpu_custom_call" | custom-call | flops 2000000000 | bytes 4000000 | tf_op jit(solution)/shard_map/pallas_call | solution.py:271
  (2 shorter events, 0.0 us)
Async XLA Ops:
  1.8 28.3 %collective-permute-start.1 = (bf16[4,2,2,64,128]{4,3,2,1,0:T(8,128)(2,1)}, bf16[4,2,2,64,128]{4,3,2,1,0:T(8,128)(2,1)S(1)}, u32[]{:S(2)}, u32[]{:S(2)}) collective-permute-start(bf16[4,2,2,64,128]{4,3,2,1,0:T(8,128)(2,1)} %get-tuple-element.14.own_ref), channel_id=1, source_target_pairs={{0,1},{1,2},{2,3},{3,4},{4,5},{5,6},{6,7},{7,8},{8,9},{9,10},{10,1... | collective-permute-start | bytes 786440 | tf_op jit(solution)/shard_map/ppermute | solution.py:237
  6.2 24.0 %collective-permute-start = (bf16[4,2,2,64,128]{4,3,2,1,0:T(8,128)(2,1)}, bf16[4,2,2,64,128]{4,3,2,1,0:T(8,128)(2,1)S(1)}, u32[]{:S(2)}, u32[]{:S(2)}) collective-permute-start(bf16[4,2,2,64,128]{4,3,2,1,0:T(8,128)(2,1)} %get-tuple-element.14.own_ref), channel_id=1, source_target_pairs={{0,4},{1,5},{2,6},{3,7},{4,8},{5,9},{6,10},{7,11},{8,12},{9,13},{1... | collective-permute-start | bytes 786440 | tf_op jit(solution)/shard_map/ppermute | solution.py:237
  9.4 20.7 %all-to-all-start = ((bf16[32,32,128]{2,1,0:T(8,128)(2,1)}), bf16[32,32,128]{2,1,0:T(8,128)(2,1)S(1)}, u32[]{:S(2)}, u32[]{:S(2)}) async-start(bf16[32,32,128]{2,1,0:T(8,128)(2,1)} %get-tuple-element.15), calls=%async_computation | async-start | bytes 524288 | tf_op jit(solution)/shard_map/all_to_all | solution.py:241
  30.1 0.7 copy-start.15
  30.1 0.8 copy-start.2
  30.1 0.9 copy-start.5
  52.2 7.0 %collective-permute-start.2 = (bf16[4,2,2,64,128]{4,3,2,1,0:T(8,128)(2,1)}, bf16[4,2,2,64,128]{4,3,2,1,0:T(8,128)(2,1)S(1)}, u32[]{:S(2)}, u32[]{:S(2)}) collective-permute-start(bf16[4,2,2,64,128]{4,3,2,1,0:T(8,128)(2,1)} %get-tuple-element.18), channel_id=1, source_target_pairs={{0,3},{1,0},{2,1},{3,2},{4,7},{5,4},{6,5},{7,6},{8,11},{9,8},{10,9... | collective-permute-start | bytes 786440 | tf_op jit(solution)/shard_map/ppermute | solution.py:258
  52.8 15.1 %collective-permute-start.3 = (bf16[4,2,2,64,128]{4,3,2,1,0:T(8,128)(2,1)}, bf16[4,2,2,64,128]{4,3,2,1,0:T(8,128)(2,1)S(1)}, u32[]{:S(2)}, u32[]{:S(2)}) collective-permute-start(bf16[4,2,2,64,128]{4,3,2,1,0:T(8,128)(2,1)} %get-tuple-element.19.first_ref), channel_id=1, source_target_pairs={{0,1},{1,2},{2,3},{3,4},{4,5},{5,6},{6,7},{7,8},{8,9},{9,10},{10,1... | collective-permute-start | bytes 786440 | tf_op jit(solution)/shard_map/ppermute | solution.py:237
  55.5 15.3 %all-to-all-start.2 = ((bf16[16,8,16,128]{3,2,1,0:T(8,128)(2,1)}), bf16[16,8,16,128]{3,2,1,0:T(8,128)(2,1)S(1)}, u32[]{:S(2)}, u32[]{:S(2)}) async-start(bf16[16,8,16,128]{3,2,1,0:T(8,128)(2,1)} %get-tuple-element.22), calls=%async_computation.2 | async-start | bytes 1048576 | tf_op jit(solution)/shard_map/all_to_all | solution.py:260
  59.1 8.7 %copy-start.7 = (bf16[4,2,2,64,128]{4,3,2,1,0:T(8,128)(2,1)}, bf16[4,2,2,64,128]{4,3,2,1,0:T(8,128)(2,1)S(1)}, u32[]{:S(2)}) copy-start(bf16[4,2,2,64,128]{4,3,2,1,0:T(8,128)(2,1)S(1)} %collective-permute-done.2.refs_0_) | copy-start | bytes 786436
  67.8 0.7 copy-start.9
  68.5 7.1 %copy-start.13 = (bf16[128,3584]{1,0:T(8,128)(2,1)S(1)}, bf16[128,3584]{1,0:T(8,128)(2,1)}, u32[]{:S(2)}) copy-start(bf16[128,3584]{1,0:T(8,128)(2,1)} %query_ref.1) | copy-start | bytes 2752516
  70.8 0.8 copy-start
  71.6 2.2 %copy-start.16 = (s32[4,2]{0,1:T(2,128)S(1)}, s32[4,2]{0,1:T(2,128)}, u32[]{:S(2)}) copy-start(s32[4,2]{0,1:T(2,128)} %param.11) | copy-start | bytes 100
  71.6 4.0 %copy-start.3 = (bf16[4,2,2,64,128]{4,3,2,1,0:T(8,128)(2,1)S(1)}, bf16[4,2,2,64,128]{4,3,2,1,0:T(8,128)(2,1)}, u32[]{:S(2)}) copy-start(bf16[4,2,2,64,128]{4,3,2,1,0:T(8,128)(2,1)} %get-tuple-element.19.first_ref) | copy-start | bytes 786436
  71.6 4.0 %copy-start.4 = (bf16[4,2,2,64,128]{4,3,2,1,0:T(8,128)(2,1)S(1)}, bf16[4,2,2,64,128]{4,3,2,1,0:T(8,128)(2,1)}, u32[]{:S(2)}) copy-start(bf16[4,2,2,64,128]{4,3,2,1,0:T(8,128)(2,1)} %get-tuple-element.14.own_ref) | copy-start | bytes 786436
  71.6 4.0 %copy-start.6 = (bf16[4,2,2,64,128]{4,3,2,1,0:T(8,128)(2,1)S(1)}, bf16[4,2,2,64,128]{4,3,2,1,0:T(8,128)(2,1)}, u32[]{:S(2)}) copy-start(bf16[4,2,2,64,128]{4,3,2,1,0:T(8,128)(2,1)} %copy-done.5) | copy-start | bytes 786436
  71.6 4.0 %copy-start.8 = (bf16[4,2,2,64,128]{4,3,2,1,0:T(8,128)(2,1)S(1)}, bf16[4,2,2,64,128]{4,3,2,1,0:T(8,128)(2,1)}, u32[]{:S(2)}) copy-start(bf16[4,2,2,64,128]{4,3,2,1,0:T(8,128)(2,1)} %get-tuple-element.20.refs_1_.third_ref) | copy-start | bytes 786436
  71.7 4.0 %copy-start.10 = (bf16[4,2,2,64,128]{4,3,2,1,0:T(8,128)(2,1)S(1)}, bf16[4,2,2,64,128]{4,3,2,1,0:T(8,128)(2,1)}, u32[]{:S(2)}) copy-start(bf16[4,2,2,64,128]{4,3,2,1,0:T(8,128)(2,1)} %get-tuple-element.21.refs_2_.second_ref) | copy-start | bytes 786436
  71.7 3.9 %collective-permute-start.4 = (bf16[16,8,16,128]{3,2,1,0:T(8,128)(2,1)}, bf16[16,8,16,128]{3,2,1,0:T(8,128)(2,1)S(1)}, u32[]{:S(2)}, u32[]{:S(2)}) collective-permute-start(bf16[16,8,16,128]{3,2,1,0:T(8,128)(2,1)} %shard_map.68), channel_id=1, source_target_pairs={{0,64},{64,0},{1,65},{65,1},{2,66},{66,2},{3,67},{67,3},{4,68},{68... | collective-permute-start | bytes 1572872 | tf_op jit(solution)/shard_map/ppermute | solution.py:263
  73.9 1.8 %copy-start.14 = (s32[4,9]{1,0:T(4,128)S(1)}, s32[4,9]{1,0:T(4,128)}, u32[]{:S(2)}) copy-start(s32[4,9]{1,0:T(4,128)} %offsets_ref.1) | copy-start | bytes 436
  74.0 1.7 %copy-start.11 = (s32[4,8]{1,0:T(4,128)S(1)}, s32[4,8]{1,0:T(4,128)}, u32[]{:S(2)}) copy-start(s32[4,8]{1,0:T(4,128)} %vertical_ref.5) | copy-start | bytes 388
  75.6 0.7 copy-start.12
  76.3 1.0 %copy-start.1 = (bf16[16,8,16,128]{3,2,1,0:T(8,128)(2,1)S(1)}, bf16[16,8,16,128]{3,2,1,0:T(8,128)(2,1)}, u32[]{:S(2)}) copy-start(bf16[16,8,16,128]{3,2,1,0:T(8,128)(2,1)} %shard_map.68) | copy-start | bytes 1572868

commit v3 on v2

--- a/solution.py
+++ b/solution.py
@@ -17,14 +17,13 @@
 SIZES = (2, 2, 4, 4, 4)
 AXES = ("zh", "c", "x", "y", "zl")
 DEVICES = 256
-CHUNK = 4
-CAPACITY = 5 * CHUNK
+CHUNK = 2
+CAPACITY = 9 * CHUNK
 NEGATIVE = -1e30
 LOG2_SCALE = math.log2(math.e) * HD ** (-0.5)
 VMEM = pl.BlockSpec(memory_space=pltpu.VMEM)
 SMEM = pl.BlockSpec(memory_space=pltpu.SMEM)
 ANY = pl.BlockSpec(memory_space=pl.ANY)
-THREE_BACK = [(0, 3), (1, 0), (2, 1), (3, 2)]
 
 
 def owner_plane(block):
@@ -48,7 +47,7 @@
 
 
 def pick_owned_kernel(
-    place_ref, vertical_ref, received_ref, own_ref, fourth_ref, first_ref, out_ref, chosen_ref
+    place_ref, vertical_ref, received_ref, first_ref, fourth_ref, out_ref
 ):
     head = place_ref[0] >> 3
     for j in range(MAXV):
@@ -56,18 +55,9 @@
         piece = received_ref[owner_plane(block), block & 1]
         for copy in range(8):
             out_ref[copy, j] = piece
-    first_of_line = (place_ref[1] & 3) == 0
-
-    @pl.when(first_of_line)
-    def _():
-        chosen_ref[...] = own_ref[...]
-
-    @pl.when(jnp.logical_not(first_of_line))
-    def _():
-        chosen_ref[...] = fourth_ref[...]
-
-
-def pick_layer_kernel(place_ref, vertical_ref, received_ref, chosen_ref, first_ref, *refs):
+
+
+def pick_layer_kernel(place_ref, vertical_ref, received_ref, fourth_ref, first_ref, *refs):
     out_ref = refs[-3]
     head = place_ref[0] >> 3
     for j in range(MAXV):
@@ -233,29 +223,29 @@
     )(key, value)
 
     def shifted(array, distance):
-        route = [(i, i + distance) for i in range(DEVICES - distance)]
+        route = [(i, (i + distance) % DEVICES) for i in range(DEVICES)]
         return lax.ppermute(array, AXES, route)
 
     fourth = shifted(own, 4)
     first = shifted(own, 1)
     spread = lax.all_to_all(packed, ("c", "x", "y"), 0, 0, tiled=True)
-    owned, chosen = pl.pallas_call(
+    owned = pl.pallas_call(
         pick_owned_kernel,
-        out_shape=(jax.ShapeDtypeStruct((8, MAXV, 16, HD), bf16), slab_shape),
-        in_specs=[SMEM, SMEM, VMEM, VMEM, VMEM, VMEM],
-        out_specs=(VMEM, VMEM),
-    )(place, vertical_blocks, spread.reshape(32, 2, 16, HD), own, fourth, first)
+        out_shape=jax.ShapeDtypeStruct((8, MAXV, 16, HD), bf16),
+        in_specs=[SMEM, SMEM, VMEM, VMEM, VMEM],
+        out_specs=VMEM,
+    )(place, vertical_blocks, spread.reshape(32, 2, 16, HD), first, fourth)
     layers = lax.all_to_all(owned, ("zh", "zl"), 0, 0, tiled=True)
     late = [
     ]
-    pieces, chosen, first = pl.pallas_call(
+    pieces, fourth, first = pl.pallas_call(
         pick_layer_kernel,
         out_shape=(jax.ShapeDtypeStruct((16, MAXV, 16, HD), bf16), slab_shape, slab_shape),
         in_specs=[SMEM, SMEM, VMEM, ANY, ANY] + [ANY] * len(late),
         out_specs=(VMEM, ANY, ANY),
         input_output_aliases={3: 1, 4: 2},
-    )(place, vertical_blocks, layers, chosen, first, *late)
-    third = lax.ppermute(chosen, "zl", THREE_BACK)
+    )(place, vertical_blocks, layers, fourth, first, *late)
+    third = shifted(fourth, -1)
     second = shifted(first, 1)
     near = lax.all_to_all(pieces, ("x", "y"), 0, 0, tiled=True)
     third, second = hold(third, second)

time: 87.5 us -> 83.4 us (0.953)
  starting transfers between devices: 28.6 us -> 21.7 us
  waiting for transfers between devices: 20.8 us -> 24 us
  Pallas kernels: 15.4 us -> 13.9 us
    ppermute x3 -> x4, starting transfers between devices: 10.3 us -> 5.23 us  [shifted(): return lax.ppermute(array, AXES, route)]
    ppermute x3 -> x4, waiting for transfers between devices: 8.69 us -> 12.4 us  [shifted(): return lax.ppermute(array, AXES, route)]
    pallas_call x1, Pallas kernels: 9.61 us -> 8.33 us  [local(): pl.pallas_call(attend_kernel, out_shape=jax.ShapeDtypeStruct((2 * BLOCK,...]
    ppermute x1, starting transfers between devices: 2.19 us -> 1.31 us  [local(): far = lax.ppermute(near, 'c', [(0, 1), (1, 0)])]
  transfers between devices with their start and end apart: 7 -> 7, of which waited for: 4 -> 5; matrix products, arithmetic and copies ran while one was open for 1% -> 1% of each run, Pallas kernels for 0% -> 0%
where the time goes in v3:
time: 83.4 us; the launch traced here: 82.5 us
  waiting for transfers between devices  24 us (29%)
  starting transfers between devices  21.7 us (26%)
  blocking collectives  17.8 us (21%)
  Pallas kernels  13.9 us (17%)
  local copies, waits for them, and re-layouts  4.09 us (5%)
    all_to_all x1, blocking collectives, local(): layers = lax.all_to_all(owned, ('zh', 'zl'), 0, 0, tiled=True)  17.8 us
    ppermute x4, waiting for transfers between devices, shifted(): return lax.ppermute(array, AXES, route)  12.4 us
    all_to_all x1, starting transfers between devices, local(): spread = lax.all_to_all(packed, ('c', 'x', 'y'), 0, 0, tiled=True)  11.6 us
    pallas_call x1, Pallas kernels, local(): pl.pallas_call(attend_kernel, out_shape=jax.ShapeDtypeStruct((2 * BLOCK,...  8.33 us
    all_to_all x1, waiting for transfers between devices, local(): spread = lax.all_to_all(packed, ('c', 'x', 'y'), 0, 0, tiled=True)  8.18 us
    ppermute x4, starting transfers between devices, shifted(): return lax.ppermute(array, AXES, route)  5.23 us
    unnamed x35, local copies, waits for them, and re-layouts  4.09 us
    all_to_all x1, starting transfers between devices, local(): near = lax.all_to_all(pieces, ('x', 'y'), 0, 0, tiled=True)  3.57 us
  transfers between devices with their start and end apart: 7, of which 5 were waited for; matrix products, arithmetic and copies ran while one was open for 1% of the time, Pallas kernels for 0%

profile of v3, /device:TPU:1, one launch (start us, length us, event | category | flops | bytes accessed | tf_op | source)
XLA Modules:
  0.0 82.5 jit_solution(1629514651743886043)
XLA Ops:
  0.0 1.8 %shard_map.64 = (bf16[32,32,128]{2,1,0:T(8,128)(2,1)}, bf16[4,2,2,64,128]{4,3,2,1,0:T(8,128)(2,1)}) custom-call(bf16[128,512]{1,0:T(8,128)(2,1)} %key_ref.1, bf16[128,512]{1,0:T(8,128)(2,1)} %value_ref.1), custom_call_target="tpu_custom_call" | custom-call | tf_op jit(solution)/shard_map/pallas_call | solution.py:218
  1.8 2.1 %collective-permute-start.1 = (bf16[4,2,2,64,128]{4,3,2,1,0:T(8,128)(2,1)}, bf16[4,2,2,64,128]{4,3,2,1,0:T(8,128)(2,1)S(1)}, u32[]{:S(2)}, u32[]{:S(2)}) collective-permute-start(bf16[4,2,2,64,128]{4,3,2,1,0:T(8,128)(2,1)} %get-tuple-element.12.own_ref), channel_id=1, source_target_pairs={{0,4},{1,5},{2,6},{3,7},{4,8},{5,9},{6,10},{7,11},{8,12},{9,13},{1... | collective-permute-start | bytes 786440 | tf_op jit(solution)/shard_map/ppermute | solution.py:227
  4.0 1.6 %collective-permute-start = (bf16[4,2,2,64,128]{4,3,2,1,0:T(8,128)(2,1)}, bf16[4,2,2,64,128]{4,3,2,1,0:T(8,128)(2,1)S(1)}, u32[]{:S(2)}, u32[]{:S(2)}) collective-permute-start(bf16[4,2,2,64,128]{4,3,2,1,0:T(8,128)(2,1)} %get-tuple-element.12.own_ref), channel_id=1, source_target_pairs={{0,1},{1,2},{2,3},{3,4},{4,5},{5,6},{6,7},{7,8},{8,9},{9,10},{10,1... | collective-permute-start | bytes 786440 | tf_op jit(solution)/shard_map/ppermute | solution.py:227
  5.6 11.6 %all-to-all-start = ((bf16[32,32,128]{2,1,0:T(8,128)(2,1)}), bf16[32,32,128]{2,1,0:T(8,128)(2,1)S(1)}, u32[]{:S(2)}, u32[]{:S(2)}) async-start(bf16[32,32,128]{2,1,0:T(8,128)(2,1)} %get-tuple-element.13), calls=%async_computation | async-start | bytes 524288 | tf_op jit(solution)/shard_map/all_to_all | solution.py:231
  17.2 0.6 pad_add_fusion.place_ref
  17.9 8.2 %all-to-all-done = bf16[32,32,128]{2,1,0:T(8,128)(2,1)S(1)} async-done(((bf16[32,32,128]{2,1,0:T(8,128)(2,1)}), bf16[32,32,128]{2,1,0:T(8,128)(2,1)S(1)}, u32[]{:S(2)}, u32[]{:S(2)}) %all-to-all-start) | async-done | bytes 262176 | tf_op jit(solution)/shard_map/all_to_all | solution.py:231
  26.0 0.0 copy-start.15
  26.0 0.0 collective-permute-done.1.fourth_ref
  26.0 0.0 copy-start.2
  26.0 0.0 collective-permute-done.first_ref
  26.1 0.0 copy-start.4
  26.1 0.7 copy-done.15
  26.7 0.1 copy-done.2
  26.8 0.1 copy-done.4
  26.9 1.9 %shard_map.65 = bf16[8,8,16,128]{3,2,1,0:T(8,128)(2,1)} custom-call(s32[3]{0:T(128)} %pad_add_fusion.place_ref, s32[4,8]{1,0:T(4,128)} %vertical_ref.5, bf16[32,2,16,128]{3,2,1,0:T(8,128)(2,1)} %bitcast.8, bf16[4,2,2,64,128]{4,3,2,1,0:T(8,128)(2,1)} %copy-done.4, bf16[4,2,2,64,128]{4,3,2,1,0:T(8,128)(2,1)} %copy-done.2), custom_call_target="tpu_custom_call" | custom-call | tf_op jit(solution)/shard_map/pallas_call | solution.py:232
  28.8 17.8 %all_to_all.15.received_ref = bf16[8,8,16,128]{3,2,1,0:T(8,128)(2,1)} all-to-all(bf16[8,8,16,128]{3,2,1,0:T(8,128)(2,1)} %shard_map.65), channel_id=1, replica_groups=mesh['zh'=2,'c'=2,'x'=4,'y'=4,'zl'=4] {'zh','zl'}, dimensions={0} | all-to-all | bytes 524288 | tf_op jit(solution)/shard_map/all_to_all | solution.py:238
  46.6 1.9 %shard_map.66 = (bf16[16,8,16,128]{3,2,1,0:T(8,128)(2,1)}, bf16[4,2,2,64,128]{4,3,2,1,0:T(8,128)(2,1)}, bf16[4,2,2,64,128]{4,3,2,1,0:T(8,128)(2,1)}) custom-call(s32[3]{0:T(128)} %pad_add_fusion.place_ref, s32[4,8]{1,0:T(4,128)} %vertical_ref.5, bf16[8,8,16,128]{3,2,1,0:T(8,128)(2,1)} %all_to_all.15.received_ref, ...), custom_call_target="tpu_custom_call", output_to_operand_aliasing={{1}: (3, {}), {2}: (4, {})} | custom-call | tf_op jit(solution)/shard_map/pallas_call | solution.py:241
  48.5 1.1 %collective-permute-start.2 = (bf16[4,2,2,64,128]{4,3,2,1,0:T(8,128)(2,1)}, bf16[4,2,2,64,128]{4,3,2,1,0:T(8,128)(2,1)S(1)}, u32[]{:S(2)}, u32[]{:S(2)}) collective-permute-start(bf16[4,2,2,64,128]{4,3,2,1,0:T(8,128)(2,1)} %get-tuple-element.14.fourth_ref), channel_id=1, source_target_pairs={{0,255},{1,0},{2,1},{3,2},{4,3},{5,4},{6,5},{7,6},{8,7},{9,8},{10,... | collective-permute-start | bytes 786440 | tf_op jit(solution)/shard_map/ppermute | solution.py:227
  49.6 0.4 collective-permute-start.3
  49.9 3.6 %all-to-all-start.2 = ((bf16[16,8,16,128]{3,2,1,0:T(8,128)(2,1)}), bf16[16,8,16,128]{3,2,1,0:T(8,128)(2,1)S(1)}, u32[]{:S(2)}, u32[]{:S(2)}) async-start(bf16[16,8,16,128]{3,2,1,0:T(8,128)(2,1)} %get-tuple-element.18), calls=%async_computation.2 | async-start | bytes 1048576 | tf_op jit(solution)/shard_map/all_to_all | solution.py:250
  53.5 1.3 %collective-permute-done.2.refs_0_ = bf16[4,2,2,64,128]{4,3,2,1,0:T(8,128)(2,1)S(1)} collective-permute-done((bf16[4,2,2,64,128]{4,3,2,1,0:T(8,128)(2,1)}, bf16[4,2,2,64,128]{4,3,2,1,0:T(8,128)(2,1)S(1)}, u32[]{:S(2)}, u32[]{:S(2)}) %collective-permute-start.2) | collective-permute-done | bytes 262176 | tf_op jit(solution)/shard_map/ppermute | solution.py:227
  54.8 0.0 copy-start.6
  54.8 11.1 %collective-permute-done.3.refs_1_ = bf16[4,2,2,64,128]{4,3,2,1,0:T(8,128)(2,1)S(1)} collective-permute-done((bf16[4,2,2,64,128]{4,3,2,1,0:T(8,128)(2,1)}, bf16[4,2,2,64,128]{4,3,2,1,0:T(8,128)(2,1)S(1)}, u32[]{:S(2)}, u32[]{:S(2)}) %collective-permute-start.3) | collective-permute-done | bytes 262176 | tf_op jit(solution)/shard_map/ppermute | solution.py:227
  65.9 0.0 copy-done.6
  65.9 0.0 copy-start.8
  65.9 0.7 copy-done.8
  66.6 0.0 copy-start.12
  66.6 1.8 %all-to-all-done.2.refs_0_ = bf16[16,8,16,128]{3,2,1,0:T(8,128)(2,1)S(1)} async-done(((bf16[16,8,16,128]{3,2,1,0:T(8,128)(2,1)}), bf16[16,8,16,128]{3,2,1,0:T(8,128)(2,1)S(1)}, u32[]{:S(2)}, u32[]{:S(2)}) %all-to-all-start.2) | async-done | bytes 524320 | tf_op jit(solution)/shard_map/all_to_all | solution.py:250
  68.4 0.0 copy-start
  68.4 0.8 copy-done
  69.2 0.0 copy-start.16
  69.2 0.0 copy-start.3
  69.2 0.0 copy-start.5
  69.2 0.0 copy-start.7
  69.2 0.0 copy-start.9
  69.2 0.0 copy-start.13
  69.3 1.3 %collective-permute-start.4 = (bf16[16,8,16,128]{3,2,1,0:T(8,128)(2,1)}, bf16[16,8,16,128]{3,2,1,0:T(8,128)(2,1)S(1)}, u32[]{:S(2)}, u32[]{:S(2)}) collective-permute-start(bf16[16,8,16,128]{3,2,1,0:T(8,128)(2,1)} %shard_map.68), channel_id=1, source_target_pairs={{0,64},{64,0},{1,65},{65,1},{2,66},{66,2},{3,67},{67,3},{4,68},{68... | collective-permute-start | bytes 1572872 | tf_op jit(solution)/shard_map/ppermute | solution.py:253
  70.6 0.0 copy-done.16
  70.6 0.0 copy-start.14
  70.6 0.1 copy.12.counts_ref
  70.7 0.0 copy-start.10
  70.7 1.6 %collective-permute-done.4 = bf16[16,8,16,128]{3,2,1,0:T(8,128)(2,1)S(1)} collective-permute-done((bf16[16,8,16,128]{3,2,1,0:T(8,128)(2,1)}, bf16[16,8,16,128]{3,2,1,0:T(8,128)(2,1)S(1)}, u32[]{:S(2)}, u32[]{:S(2)}) %collective-permute-start.4) | collective-permute-done | bytes 524320 | tf_op jit(solution)/shard_map/ppermute | solution.py:253
  72.3 0.0 copy-start.11
  72.3 0.0 copy-done.12
  72.3 0.0 copy-done.3
  72.3 0.0 copy-done.5
  72.3 0.0 copy-done.7
  72.3 0.0 copy-done.9
  72.4 0.0 copy-done.13
  72.4 0.0 copy-done.14
  72.4 0.0 copy-done.10
  72.4 0.6 copy-done.11
  73.0 0.0 copy-start.1
  73.0 1.0 %copy-done.1 = bf16[16,8,16,128]{3,2,1,0:T(8,128)(2,1)S(1)} copy-done((bf16[16,8,16,128]{3,2,1,0:T(8,128)(2,1)S(1)}, bf16[16,8,16,128]{3,2,1,0:T(8,128)(2,1)}, u32[]{:S(2)}) %copy-start.1) | copy-done | bytes 524312
  74.0 8.3 %shard_map.69 = bf16[128,3584]{1,0:T(8,128)(2,1)} custom-call(s32[3]{0:T(128)S(1)} %copy-done.11, s32[4,8]{1,0:T(4,128)S(1)} %copy-done.10, s32[4,9]{1,0:T(4,128)S(1)} %copy-done.14, s32[4,2]{1,0:T(4,128)S(1)} %copy.12.counts_ref, bf16[128,3584]{1,0:T(8,128)(2,1)S(1)} %copy-done.12, bf16[4,2,2,64,128]{4,3,2,1,0:T(8,128)(2,1)S(1)} %copy-done.13, ...), custom_call_target="tpu_custom_call" | custom-call | flops 2000000000 | bytes 4000000 | tf_op jit(solution)/shard_map/pallas_call | solution.py:261
  (2 shorter events, 0.0 us)
Async XLA Ops:
  1.8 24.2 %collective-permute-start.1 = (bf16[4,2,2,64,128]{4,3,2,1,0:T(8,128)(2,1)}, bf16[4,2,2,64,128]{4,3,2,1,0:T(8,128)(2,1)S(1)}, u32[]{:S(2)}, u32[]{:S(2)}) collective-permute-start(bf16[4,2,2,64,128]{4,3,2,1,0:T(8,128)(2,1)} %get-tuple-element.12.own_ref), channel_id=1, source_target_pairs={{0,4},{1,5},{2,6},{3,7},{4,8},{5,9},{6,10},{7,11},{8,12},{9,13},{1... | collective-permute-start | bytes 786440 | tf_op jit(solution)/shard_map/ppermute | solution.py:227
  4.0 22.1 %collective-permute-start = (bf16[4,2,2,64,128]{4,3,2,1,0:T(8,128)(2,1)}, bf16[4,2,2,64,128]{4,3,2,1,0:T(8,128)(2,1)S(1)}, u32[]{:S(2)}, u32[]{:S(2)}) collective-permute-start(bf16[4,2,2,64,128]{4,3,2,1,0:T(8,128)(2,1)} %get-tuple-element.12.own_ref), channel_id=1, source_target_pairs={{0,1},{1,2},{2,3},{3,4},{4,5},{5,6},{6,7},{7,8},{8,9},{9,10},{10,1... | collective-permute-start | bytes 786440 | tf_op jit(solution)/shard_map/ppermute | solution.py:227
  5.6 20.4 %all-to-all-start = ((bf16[32,32,128]{2,1,0:T(8,128)(2,1)}), bf16[32,32,128]{2,1,0:T(8,128)(2,1)S(1)}, u32[]{:S(2)}, u32[]{:S(2)}) async-start(bf16[32,32,128]{2,1,0:T(8,128)(2,1)} %get-tuple-element.13), calls=%async_computation | async-start | bytes 524288 | tf_op jit(solution)/shard_map/all_to_all | solution.py:231
  26.0 0.7 copy-start.15
  26.0 0.8 copy-start.2
  26.1 0.8 %copy-start.4 = (bf16[4,2,2,64,128]{4,3,2,1,0:T(8,128)(2,1)}, bf16[4,2,2,64,128]{4,3,2,1,0:T(8,128)(2,1)S(1)}, u32[]{:S(2)}) copy-start(bf16[4,2,2,64,128]{4,3,2,1,0:T(8,128)(2,1)S(1)} %collective-permute-done.first_ref) | copy-start | bytes 786436
  48.5 6.3 %collective-permute-start.2 = (bf16[4,2,2,64,128]{4,3,2,1,0:T(8,128)(2,1)}, bf16[4,2,2,64,128]{4,3,2,1,0:T(8,128)(2,1)S(1)}, u32[]{:S(2)}, u32[]{:S(2)}) collective-permute-start(bf16[4,2,2,64,128]{4,3,2,1,0:T(8,128)(2,1)} %get-tuple-element.14.fourth_ref), channel_id=1, source_target_pairs={{0,255},{1,0},{2,1},{3,2},{4,3},{5,4},{6,5},{7,6},{8,7},{9,8},{10,... | collective-permute-start | bytes 786440 | tf_op jit(solution)/shard_map/ppermute | solution.py:227
  49.6 16.3 %collective-permute-start.3 = (bf16[4,2,2,64,128]{4,3,2,1,0:T(8,128)(2,1)}, bf16[4,2,2,64,128]{4,3,2,1,0:T(8,128)(2,1)S(1)}, u32[]{:S(2)}, u32[]{:S(2)}) collective-permute-start(bf16[4,2,2,64,128]{4,3,2,1,0:T(8,128)(2,1)} %get-tuple-element.15.first_ref), channel_id=1, source_target_pairs={{0,1},{1,2},{2,3},{3,4},{4,5},{5,6},{6,7},{7,8},{8,9},{9,10},{10,1... | collective-permute-start | bytes 786440 | tf_op jit(solution)/shard_map/ppermute | solution.py:227
  49.9 18.5 %all-to-all-start.2 = ((bf16[16,8,16,128]{3,2,1,0:T(8,128)(2,1)}), bf16[16,8,16,128]{3,2,1,0:T(8,128)(2,1)S(1)}, u32[]{:S(2)}, u32[]{:S(2)}) async-start(bf16[16,8,16,128]{3,2,1,0:T(8,128)(2,1)} %get-tuple-element.18), calls=%async_computation.2 | async-start | bytes 1048576 | tf_op jit(solution)/shard_map/all_to_all | solution.py:250
  54.8 11.1 %copy-start.6 = (bf16[4,2,2,64,128]{4,3,2,1,0:T(8,128)(2,1)}, bf16[4,2,2,64,128]{4,3,2,1,0:T(8,128)(2,1)S(1)}, u32[]{:S(2)}) copy-start(bf16[4,2,2,64,128]{4,3,2,1,0:T(8,128)(2,1)S(1)} %collective-permute-done.2.refs_0_) | copy-start | bytes 786436
  65.9 0.7 copy-start.8
  66.6 5.7 %copy-start.12 = (bf16[128,3584]{1,0:T(8,128)(2,1)S(1)}, bf16[128,3584]{1,0:T(8,128)(2,1)}, u32[]{:S(2)}) copy-start(bf16[128,3584]{1,0:T(8,128)(2,1)} %query_ref.1) | copy-start | bytes 2752516
  68.4 0.8 copy-start
  69.2 1.4 %copy-start.16 = (s32[4,2]{0,1:T(2,128)S(1)}, s32[4,2]{0,1:T(2,128)}, u32[]{:S(2)}) copy-start(s32[4,2]{0,1:T(2,128)} %param.11) | copy-start | bytes 100
  69.2 3.1 %copy-start.3 = (bf16[4,2,2,64,128]{4,3,2,1,0:T(8,128)(2,1)S(1)}, bf16[4,2,2,64,128]{4,3,2,1,0:T(8,128)(2,1)}, u32[]{:S(2)}) copy-start(bf16[4,2,2,64,128]{4,3,2,1,0:T(8,128)(2,1)} %get-tuple-element.14.fourth_ref) | copy-start | bytes 786436
  69.2 3.1 %copy-start.5 = (bf16[4,2,2,64,128]{4,3,2,1,0:T(8,128)(2,1)S(1)}, bf16[4,2,2,64,128]{4,3,2,1,0:T(8,128)(2,1)}, u32[]{:S(2)}) copy-start(bf16[4,2,2,64,128]{4,3,2,1,0:T(8,128)(2,1)} %get-tuple-element.15.first_ref) | copy-start | bytes 786436
  69.2 3.1 %copy-start.7 = (bf16[4,2,2,64,128]{4,3,2,1,0:T(8,128)(2,1)S(1)}, bf16[4,2,2,64,128]{4,3,2,1,0:T(8,128)(2,1)}, u32[]{:S(2)}) copy-start(bf16[4,2,2,64,128]{4,3,2,1,0:T(8,128)(2,1)} %get-tuple-element.16.refs_1_.third_ref) | copy-start | bytes 786436
  69.2 3.1 %copy-start.9 = (bf16[4,2,2,64,128]{4,3,2,1,0:T(8,128)(2,1)S(1)}, bf16[4,2,2,64,128]{4,3,2,1,0:T(8,128)(2,1)}, u32[]{:S(2)}) copy-start(bf16[4,2,2,64,128]{4,3,2,1,0:T(8,128)(2,1)} %get-tuple-element.17.refs_2_.second_ref) | copy-start | bytes 786436
  69.2 3.1 %copy-start.13 = (bf16[4,2,2,64,128]{4,3,2,1,0:T(8,128)(2,1)S(1)}, bf16[4,2,2,64,128]{4,3,2,1,0:T(8,128)(2,1)}, u32[]{:S(2)}) copy-start(bf16[4,2,2,64,128]{4,3,2,1,0:T(8,128)(2,1)} %get-tuple-element.12.own_ref) | copy-start | bytes 786436
  69.3 3.1 %collective-permute-start.4 = (bf16[16,8,16,128]{3,2,1,0:T(8,128)(2,1)}, bf16[16,8,16,128]{3,2,1,0:T(8,128)(2,1)S(1)}, u32[]{:S(2)}, u32[]{:S(2)}) collective-permute-start(bf16[16,8,16,128]{3,2,1,0:T(8,128)(2,1)} %shard_map.68), channel_id=1, source_target_pairs={{0,64},{64,0},{1,65},{65,1},{2,66},{66,2},{3,67},{67,3},{4,68},{68... | collective-permute-start | bytes 1572872 | tf_op jit(solution)/shard_map/ppermute | solution.py:253
  70.6 1.8 %copy-start.14 = (s32[4,9]{1,0:T(4,128)S(1)}, s32[4,9]{1,0:T(4,128)}, u32[]{:S(2)}) copy-start(s32[4,9]{1,0:T(4,128)} %offsets_ref.1) | copy-start | bytes 436
  70.7 1.7 %copy-start.10 = (s32[4,8]{1,0:T(4,128)S(1)}, s32[4,8]{1,0:T(4,128)}, u32[]{:S(2)}) copy-start(s32[4,8]{1,0:T(4,128)} %vertical_ref.5) | copy-start | bytes 388
  72.3 0.6 copy-start.11
  73.0 1.0 %copy-start.1 = (bf16[16,8,16,128]{3,2,1,0:T(8,128)(2,1)S(1)}, bf16[16,8,16,128]{3,2,1,0:T(8,128)(2,1)}, u32[]{:S(2)}) copy-start(bf16[16,8,16,128]{3,2,1,0:T(8,128)(2,1)} %shard_map.68) | copy-start | bytes 1572868

commit v4 on v3

--- a/solution.py
+++ b/solution.py
@@ -207,6 +207,9 @@
         in_specs=[ANY] * (1 + len(others)),
         out_specs=ANY,
         input_output_aliases={0: 0},
+        cost_estimate=pl.CostEstimate(
+            flops=40_000_000_000, bytes_accessed=1_000_000, transcendentals=0
+        ),
     )(array, *others)
 
 
@@ -249,7 +252,7 @@
     second = shifted(first, 1)
     near = lax.all_to_all(pieces, ("x", "y"), 0, 0, tiled=True)
     third, second = hold(third, second)
-    near = after(near, third, second)
+    place = after(place, third, second)
     far = lax.ppermute(near, "c", [(0, 1), (1, 0)])
 
     pair_shape = (KVH, 2, 4, MAXV, 16, HD)

time: 83.4 us -> 81 us (0.971)
  local copies, waits for them, and re-layouts: 4.09 us -> 2.21 us
    unnamed x35 -> x31, local copies, waits for them, and re-layouts: 4.09 us -> 2.21 us
where the time goes in v4:
time: 81 us; the launch traced here: 80.7 us
  waiting for transfers between devices  23.8 us (29%)
  starting transfers between devices  21.5 us (27%)
  blocking collectives  17.8 us (22%)
  Pallas kernels  14.5 us (18%)
  local copies, waits for them, and re-layouts  2.21 us (3%)
    all_to_all x1, blocking collectives, local(): layers = lax.all_to_all(owned, ('zh', 'zl'), 0, 0, tiled=True)  17.8 us
    ppermute x4, waiting for transfers between devices, shifted(): return lax.ppermute(array, AXES, route)  12.2 us
    all_to_all x1, starting transfers between devices, local(): spread = lax.all_to_all(packed, ('c', 'x', 'y'), 0, 0, tiled=True)  11.6 us
    pallas_call x1, Pallas kernels, local(): pl.pallas_call(attend_kernel, out_shape=jax.ShapeDtypeStruct((2 * BLOCK,...  8.95 us
    all_to_all x1, waiting for transfers between devices, local(): spread = lax.all_to_all(packed, ('c', 'x', 'y'), 0, 0, tiled=True)  8.24 us
    ppermute x4, starting transfers between devices, shifted(): return lax.ppermute(array, AXES, route)  5.23 us
    all_to_all x1, starting transfers between devices, local(): near = lax.all_to_all(pieces, ('x', 'y'), 0, 0, tiled=True)  3.57 us
    unnamed x31, local copies, waits for them, and re-layouts  2.21 us
  transfers between devices with their start and end apart: 7, of which 5 were waited for; matrix products, arithmetic and copies ran while one was open for 1% of the time, Pallas kernels for 0%

profile of v4, /device:TPU:1, one launch (start us, length us, event | category | flops | bytes accessed | tf_op | source)
XLA Modules:
  0.0 80.7 jit_solution(15742479574497820109)
XLA Ops:
  0.0 1.8 %shard_map.64 = (bf16[32,32,128]{2,1,0:T(8,128)(2,1)}, bf16[4,2,2,64,128]{4,3,2,1,0:T(8,128)(2,1)}) custom-call(bf16[128,512]{1,0:T(8,128)(2,1)} %key_ref.1, bf16[128,512]{1,0:T(8,128)(2,1)} %value_ref.1), custom_call_target="tpu_custom_call" | custom-call | tf_op jit(solution)/shard_map/pallas_call | solution.py:221
  1.8 2.1 %collective-permute-start.1 = (bf16[4,2,2,64,128]{4,3,2,1,0:T(8,128)(2,1)}, bf16[4,2,2,64,128]{4,3,2,1,0:T(8,128)(2,1)S(1)}, u32[]{:S(2)}, u32[]{:S(2)}) collective-permute-start(bf16[4,2,2,64,128]{4,3,2,1,0:T(8,128)(2,1)} %get-tuple-element.13.own_ref), channel_id=1, source_target_pairs={{0,4},{1,5},{2,6},{3,7},{4,8},{5,9},{6,10},{7,11},{8,12},{9,13},{1... | collective-permute-start | bytes 786440 | tf_op jit(solution)/shard_map/ppermute | solution.py:230
  4.0 1.6 %collective-permute-start = (bf16[4,2,2,64,128]{4,3,2,1,0:T(8,128)(2,1)}, bf16[4,2,2,64,128]{4,3,2,1,0:T(8,128)(2,1)S(1)}, u32[]{:S(2)}, u32[]{:S(2)}) collective-permute-start(bf16[4,2,2,64,128]{4,3,2,1,0:T(8,128)(2,1)} %get-tuple-element.13.own_ref), channel_id=1, source_target_pairs={{0,1},{1,2},{2,3},{3,4},{4,5},{5,6},{6,7},{7,8},{8,9},{9,10},{10,1... | collective-permute-start | bytes 786440 | tf_op jit(solution)/shard_map/ppermute | solution.py:230
  5.6 11.6 %all-to-all-start = ((bf16[32,32,128]{2,1,0:T(8,128)(2,1)}), bf16[32,32,128]{2,1,0:T(8,128)(2,1)S(1)}, u32[]{:S(2)}, u32[]{:S(2)}) async-start(bf16[32,32,128]{2,1,0:T(8,128)(2,1)} %get-tuple-element.12), calls=%async_computation | async-start | bytes 524288 | tf_op jit(solution)/shard_map/all_to_all | solution.py:234
  17.2 0.6 pad_add_fusion.place_ref.refs_0_
  17.8 8.2 %all-to-all-done = bf16[32,32,128]{2,1,0:T(8,128)(2,1)S(1)} async-done(((bf16[32,32,128]{2,1,0:T(8,128)(2,1)}), bf16[32,32,128]{2,1,0:T(8,128)(2,1)S(1)}, u32[]{:S(2)}, u32[]{:S(2)}) %all-to-all-start) | async-done | bytes 262176 | tf_op jit(solution)/shard_map/all_to_all | solution.py:234
  26.0 0.0 copy-start.13
  26.0 0.0 collective-permute-done.1.fourth_ref
  26.0 0.0 copy-start
  26.0 0.0 collective-permute-done.first_ref
  26.0 0.0 copy-start.2
  26.1 0.7 copy-done.13
  26.7 0.1 copy-done
  26.8 0.1 copy-done.2
  26.9 1.9 %shard_map.65 = bf16[8,8,16,128]{3,2,1,0:T(8,128)(2,1)} custom-call(s32[3]{0:T(128)} %pad_add_fusion.place_ref.refs_0_, s32[4,8]{1,0:T(4,128)} %vertical_ref.5, bf16[32,2,16,128]{3,2,1,0:T(8,128)(2,1)} %bitcast.8, bf16[4,2,2,64,128]{4,3,2,1,0:T(8,128)(2,1)} %copy-done.2, bf16[4,2,2,64,128]{4,3,2,1,0:T(8,128)(2,1)} %copy-done), custom_call_target="tpu_custom_call" | custom-call | tf_op jit(solution)/shard_map/pallas_call | solution.py:235
  28.8 17.8 %all_to_all.15.received_ref = bf16[8,8,16,128]{3,2,1,0:T(8,128)(2,1)} all-to-all(bf16[8,8,16,128]{3,2,1,0:T(8,128)(2,1)} %shard_map.65), channel_id=1, replica_groups=mesh['zh'=2,'c'=2,'x'=4,'y'=4,'zl'=4] {'zh','zl'}, dimensions={0} | all-to-all | bytes 524288 | tf_op jit(solution)/shard_map/all_to_all | solution.py:241
  46.6 1.9 %shard_map.66 = (bf16[16,8,16,128]{3,2,1,0:T(8,128)(2,1)}, bf16[4,2,2,64,128]{4,3,2,1,0:T(8,128)(2,1)}, bf16[4,2,2,64,128]{4,3,2,1,0:T(8,128)(2,1)}) custom-call(s32[3]{0:T(128)} %pad_add_fusion.place_ref.refs_0_, s32[4,8]{1,0:T(4,128)} %vertical_ref.5, ...), custom_call_target="tpu_custom_call", output_to_operand_aliasing={{1}: (3, {}), {2}: (4, {})} | custom-call | tf_op jit(solution)/shard_map/pallas_call | solution.py:244
  48.5 0.0 copy-start.14
  48.5 1.1 %collective-permute-start.2 = (bf16[4,2,2,64,128]{4,3,2,1,0:T(8,128)(2,1)}, bf16[4,2,2,64,128]{4,3,2,1,0:T(8,128)(2,1)S(1)}, u32[]{:S(2)}, u32[]{:S(2)}) collective-permute-start(bf16[4,2,2,64,128]{4,3,2,1,0:T(8,128)(2,1)} %get-tuple-element.14.fourth_ref), channel_id=1, source_target_pairs={{0,255},{1,0},{2,1},{3,2},{4,3},{5,4},{6,5},{7,6},{8,7},{9,8},{10,... | collective-permute-start | bytes 786440 | tf_op jit(solution)/shard_map/ppermute | solution.py:230
  49.6 0.4 collective-permute-start.3
  49.9 0.0 copy-done.14
  49.9 0.1 copy.12.counts_ref
  50.0 3.6 %all-to-all-start.2 = ((bf16[16,8,16,128]{3,2,1,0:T(8,128)(2,1)}), bf16[16,8,16,128]{3,2,1,0:T(8,128)(2,1)S(1)}, u32[]{:S(2)}, u32[]{:S(2)}) async-start(bf16[16,8,16,128]{3,2,1,0:T(8,128)(2,1)} %get-tuple-element.18), calls=%async_computation.2 | async-start | bytes 1048576 | tf_op jit(solution)/shard_map/all_to_all | solution.py:253
  53.6 1.2 %collective-permute-done.2.refs_0_ = bf16[4,2,2,64,128]{4,3,2,1,0:T(8,128)(2,1)S(1)} collective-permute-done((bf16[4,2,2,64,128]{4,3,2,1,0:T(8,128)(2,1)}, bf16[4,2,2,64,128]{4,3,2,1,0:T(8,128)(2,1)S(1)}, u32[]{:S(2)}, u32[]{:S(2)}) %collective-permute-start.2) | collective-permute-done | bytes 262176 | tf_op jit(solution)/shard_map/ppermute | solution.py:230
  54.8 0.0 copy-start.8
  54.8 11.0 %collective-permute-done.3.refs_1_ = bf16[4,2,2,64,128]{4,3,2,1,0:T(8,128)(2,1)S(1)} collective-permute-done((bf16[4,2,2,64,128]{4,3,2,1,0:T(8,128)(2,1)}, bf16[4,2,2,64,128]{4,3,2,1,0:T(8,128)(2,1)S(1)}, u32[]{:S(2)}, u32[]{:S(2)}) %collective-permute-start.3) | collective-permute-done | bytes 262176 | tf_op jit(solution)/shard_map/ppermute | solution.py:230
  65.8 0.0 copy-done.8
  65.8 0.0 copy-start.10
  65.8 0.7 copy-done.10
  66.5 2.0 %all-to-all-done.2 = bf16[16,8,16,128]{3,2,1,0:T(8,128)(2,1)S(1)} async-done(((bf16[16,8,16,128]{3,2,1,0:T(8,128)(2,1)}), bf16[16,8,16,128]{3,2,1,0:T(8,128)(2,1)S(1)}, u32[]{:S(2)}, u32[]{:S(2)}) %all-to-all-start.2) | async-done | bytes 524320 | tf_op jit(solution)/shard_map/all_to_all | solution.py:253
  68.4 1.0 %collective-permute-start.4 = (bf16[16,8,16,128]{3,2,1,0:T(8,128)(2,1)S(1)}, bf16[16,8,16,128]{3,2,1,0:T(8,128)(2,1)S(1)}, u32[]{:S(2)}, u32[]{:S(2)}) collective-permute-start(bf16[16,8,16,128]{3,2,1,0:T(8,128)(2,1)S(1)} %all-to-all-done.2), channel_id=1, source_target_pairs={{0,64},{64,0},{1,65},{65,1},{2,66},{66,2},{3,67},{67,3},{4,68},{68... | collective-permute-start | bytes 1572872 | tf_op jit(solution)/shard_map/ppermute | solution.py:256
  69.5 0.0 copy-start.1
  69.5 0.0 copy-start.3
  69.5 0.0 copy-start.6
  69.5 0.0 copy-start.7
  69.5 0.0 copy-start.9
  69.5 0.0 copy-start.11
  69.5 0.0 copy-start.12
  69.5 0.0 copy-start.4
  69.5 1.5 %collective-permute-done.4 = bf16[16,8,16,128]{3,2,1,0:T(8,128)(2,1)S(1)} collective-permute-done((bf16[16,8,16,128]{3,2,1,0:T(8,128)(2,1)S(1)}, bf16[16,8,16,128]{3,2,1,0:T(8,128)(2,1)S(1)}, u32[]{:S(2)}, u32[]{:S(2)}) %collective-permute-start.4) | collective-permute-done | bytes 524320 | tf_op jit(solution)/shard_map/ppermute | solution.py:256
  71.0 0.0 copy-start.5
  71.0 0.0 copy-done.1
  71.0 0.0 copy-done.3
  71.0 0.0 copy-done.6
  71.0 0.0 copy-done.7
  71.0 0.0 copy-done.9
  71.0 0.0 copy-done.11
  71.1 0.0 copy-done.12
  71.1 0.0 copy-done.4
  71.1 0.5 copy-done.5
  71.6 8.9 %shard_map.69 = bf16[128,3584]{1,0:T(8,128)(2,1)} custom-call(s32[3]{0:T(128)S(1)} %copy-done.5, s32[4,8]{1,0:T(4,128)S(1)} %copy-done.4, s32[4,9]{1,0:T(4,128)S(1)} %copy-done.12, s32[4,2]{1,0:T(4,128)S(1)} %copy.12.counts_ref, bf16[128,3584]{1,0:T(8,128)(2,1)S(1)} %copy-done.6, bf16[4,2,2,64,128]{4,3,2,1,0:T(8,128)(2,1)S(1)} %copy-done.7, ...), custom_call_target="tpu_custom_call" | custom-call | flops 2000000000 | bytes 4000000 | tf_op jit(solution)/shard_map/pallas_call | solution.py:264
  (2 shorter events, 0.0 us)
Async XLA Ops:
  1.8 24.2 %collective-permute-start.1 = (bf16[4,2,2,64,128]{4,3,2,1,0:T(8,128)(2,1)}, bf16[4,2,2,64,128]{4,3,2,1,0:T(8,128)(2,1)S(1)}, u32[]{:S(2)}, u32[]{:S(2)}) collective-permute-start(bf16[4,2,2,64,128]{4,3,2,1,0:T(8,128)(2,1)} %get-tuple-element.13.own_ref), channel_id=1, source_target_pairs={{0,4},{1,5},{2,6},{3,7},{4,8},{5,9},{6,10},{7,11},{8,12},{9,13},{1... | collective-permute-start | bytes 786440 | tf_op jit(solution)/shard_map/ppermute | solution.py:230
  4.0 22.1 %collective-permute-start = (bf16[4,2,2,64,128]{4,3,2,1,0:T(8,128)(2,1)}, bf16[4,2,2,64,128]{4,3,2,1,0:T(8,128)(2,1)S(1)}, u32[]{:S(2)}, u32[]{:S(2)}) collective-permute-start(bf16[4,2,2,64,128]{4,3,2,1,0:T(8,128)(2,1)} %get-tuple-element.13.own_ref), channel_id=1, source_target_pairs={{0,1},{1,2},{2,3},{3,4},{4,5},{5,6},{6,7},{7,8},{8,9},{9,10},{10,1... | collective-permute-start | bytes 786440 | tf_op jit(solution)/shard_map/ppermute | solution.py:230
  5.6 20.4 %all-to-all-start = ((bf16[32,32,128]{2,1,0:T(8,128)(2,1)}), bf16[32,32,128]{2,1,0:T(8,128)(2,1)S(1)}, u32[]{:S(2)}, u32[]{:S(2)}) async-start(bf16[32,32,128]{2,1,0:T(8,128)(2,1)} %get-tuple-element.12), calls=%async_computation | async-start | bytes 524288 | tf_op jit(solution)/shard_map/all_to_all | solution.py:234
  26.0 0.7 copy-start.13
  26.0 0.8 copy-start
  26.0 0.8 %copy-start.2 = (bf16[4,2,2,64,128]{4,3,2,1,0:T(8,128)(2,1)}, bf16[4,2,2,64,128]{4,3,2,1,0:T(8,128)(2,1)S(1)}, u32[]{:S(2)}) copy-start(bf16[4,2,2,64,128]{4,3,2,1,0:T(8,128)(2,1)S(1)} %collective-permute-done.first_ref) | copy-start | bytes 786436
  48.5 1.5 %copy-start.14 = (s32[4,2]{0,1:T(2,128)S(1)}, s32[4,2]{0,1:T(2,128)}, u32[]{:S(2)}) copy-start(s32[4,2]{0,1:T(2,128)} %param.11) | copy-start | bytes 100
  48.5 6.3 %collective-permute-start.2 = (bf16[4,2,2,64,128]{4,3,2,1,0:T(8,128)(2,1)}, bf16[4,2,2,64,128]{4,3,2,1,0:T(8,128)(2,1)S(1)}, u32[]{:S(2)}, u32[]{:S(2)}) collective-permute-start(bf16[4,2,2,64,128]{4,3,2,1,0:T(8,128)(2,1)} %get-tuple-element.14.fourth_ref), channel_id=1, source_target_pairs={{0,255},{1,0},{2,1},{3,2},{4,3},{5,4},{6,5},{7,6},{8,7},{9,8},{10,... | collective-permute-start | bytes 786440 | tf_op jit(solution)/shard_map/ppermute | solution.py:230
  49.6 16.2 %collective-permute-start.3 = (bf16[4,2,2,64,128]{4,3,2,1,0:T(8,128)(2,1)}, bf16[4,2,2,64,128]{4,3,2,1,0:T(8,128)(2,1)S(1)}, u32[]{:S(2)}, u32[]{:S(2)}) collective-permute-start(bf16[4,2,2,64,128]{4,3,2,1,0:T(8,128)(2,1)} %get-tuple-element.15.first_ref), channel_id=1, source_target_pairs={{0,1},{1,2},{2,3},{3,4},{4,5},{5,6},{6,7},{7,8},{8,9},{9,10},{10,1... | collective-permute-start | bytes 786440 | tf_op jit(solution)/shard_map/ppermute | solution.py:230
  50.0 18.4 %all-to-all-start.2 = ((bf16[16,8,16,128]{3,2,1,0:T(8,128)(2,1)}), bf16[16,8,16,128]{3,2,1,0:T(8,128)(2,1)S(1)}, u32[]{:S(2)}, u32[]{:S(2)}) async-start(bf16[16,8,16,128]{3,2,1,0:T(8,128)(2,1)} %get-tuple-element.18), calls=%async_computation.2 | async-start | bytes 1048576 | tf_op jit(solution)/shard_map/all_to_all | solution.py:253
  54.8 11.0 %copy-start.8 = (bf16[4,2,2,64,128]{4,3,2,1,0:T(8,128)(2,1)}, bf16[4,2,2,64,128]{4,3,2,1,0:T(8,128)(2,1)S(1)}, u32[]{:S(2)}) copy-start(bf16[4,2,2,64,128]{4,3,2,1,0:T(8,128)(2,1)S(1)} %collective-permute-done.2.refs_0_) | copy-start | bytes 786436
  65.8 0.7 copy-start.10
  68.4 2.6 %collective-permute-start.4 = (bf16[16,8,16,128]{3,2,1,0:T(8,128)(2,1)S(1)}, bf16[16,8,16,128]{3,2,1,0:T(8,128)(2,1)S(1)}, u32[]{:S(2)}, u32[]{:S(2)}) collective-permute-start(bf16[16,8,16,128]{3,2,1,0:T(8,128)(2,1)S(1)} %all-to-all-done.2), channel_id=1, source_target_pairs={{0,64},{64,0},{1,65},{65,1},{2,66},{66,2},{3,67},{67,3},{4,68},{68... | collective-permute-start | bytes 1572872 | tf_op jit(solution)/shard_map/ppermute | solution.py:256
  69.5 1.5 %copy-start.1 = (bf16[4,2,2,64,128]{4,3,2,1,0:T(8,128)(2,1)S(1)}, bf16[4,2,2,64,128]{4,3,2,1,0:T(8,128)(2,1)}, u32[]{:S(2)}) copy-start(bf16[4,2,2,64,128]{4,3,2,1,0:T(8,128)(2,1)} %get-tuple-element.14.fourth_ref) | copy-start | bytes 786436
  69.5 1.5 %copy-start.3 = (bf16[4,2,2,64,128]{4,3,2,1,0:T(8,128)(2,1)S(1)}, bf16[4,2,2,64,128]{4,3,2,1,0:T(8,128)(2,1)}, u32[]{:S(2)}) copy-start(bf16[4,2,2,64,128]{4,3,2,1,0:T(8,128)(2,1)} %get-tuple-element.15.first_ref) | copy-start | bytes 786436
  69.5 1.5 %copy-start.6 = (bf16[128,3584]{1,0:T(8,128)(2,1)S(1)}, bf16[128,3584]{1,0:T(8,128)(2,1)}, u32[]{:S(2)}) copy-start(bf16[128,3584]{1,0:T(8,128)(2,1)} %query_ref.1) | copy-start | bytes 2752516
  69.5 1.5 %copy-start.7 = (bf16[4,2,2,64,128]{4,3,2,1,0:T(8,128)(2,1)S(1)}, bf16[4,2,2,64,128]{4,3,2,1,0:T(8,128)(2,1)}, u32[]{:S(2)}) copy-start(bf16[4,2,2,64,128]{4,3,2,1,0:T(8,128)(2,1)} %get-tuple-element.13.own_ref) | copy-start | bytes 786436
  69.5 1.6 %copy-start.9 = (bf16[4,2,2,64,128]{4,3,2,1,0:T(8,128)(2,1)S(1)}, bf16[4,2,2,64,128]{4,3,2,1,0:T(8,128)(2,1)}, u32[]{:S(2)}) copy-start(bf16[4,2,2,64,128]{4,3,2,1,0:T(8,128)(2,1)} %get-tuple-element.16.refs_1_.third_ref) | copy-start | bytes 786436
  69.5 1.6 %copy-start.11 = (bf16[4,2,2,64,128]{4,3,2,1,0:T(8,128)(2,1)S(1)}, bf16[4,2,2,64,128]{4,3,2,1,0:T(8,128)(2,1)}, u32[]{:S(2)}) copy-start(bf16[4,2,2,64,128]{4,3,2,1,0:T(8,128)(2,1)} %get-tuple-element.17.refs_2_.second_ref) | copy-start | bytes 786436
  69.5 1.6 %copy-start.12 = (s32[4,9]{1,0:T(4,128)S(1)}, s32[4,9]{1,0:T(4,128)}, u32[]{:S(2)}) copy-start(s32[4,9]{1,0:T(4,128)} %offsets_ref.1) | copy-start | bytes 436
  69.5 1.5 %copy-start.4 = (s32[4,8]{1,0:T(4,128)S(1)}, s32[4,8]{1,0:T(4,128)}, u32[]{:S(2)}) copy-start(s32[4,8]{1,0:T(4,128)} %vertical_ref.5) | copy-start | bytes 388
  71.0 0.6 copy-start.5
